TPU v7x, 32 devices: a whole 2x2x4 slice. The times are simulated.
32 devices in a mesh: group: 2 (over y), ctx: 4 (over z), smp: 2 (over x), head: 2 (over core).
Axes of the slice: x: 2, y: 2, z: 4, core: 2. Of those that a mesh axis runs over, the one named last changes fastest.
Arguments:
- queries: bfloat16 [512, 2, 4096], P(('group', 'smp'), 'head'), parts along dimension 0, may hold values from -8 to 8
- prefix_cache: bfloat16 [2, 8192, 2, 512], P(None, ('group', 'ctx'), 'head'), parts along dimension 1, may hold values from -8 to 8
- suffix_cache: bfloat16 [2, 512, 128, 2, 512], P(None, ('group', 'ctx', 'smp'), None, 'head'), parts along dimension 1, may hold values from -8 to 8
- suffix_length: int32 [512], P(('group', 'smp')), parts along dimension 0, may hold values from 1 to 128, as said below
- cache_sample: int32 [512], P('group'), parts along dimension 0, may hold values from 0 to 255, as said below
- residual: bfloat16 [512, 8192], P(('group', 'ctx', 'head'), 'smp'), parts along dimension 0, may hold values from -6 to 6
- w_out: bfloat16 [2, 4096, 8192], P('head', 'ctx', 'smp'), may hold values from -0.75 to 0.75
- norm_gain: float32 [8192], P('smp'), may hold values from 0.1 to 1.9
- gate_matrix: bfloat16 [8192, 16384], P('smp', ('ctx', 'head')), may hold values from -0.0625 to 0.0625
- w_up: bfloat16 [8192, 16384], P('smp', ('ctx', 'head')), may hold values from -0.0625 to 0.0625
- w_down: bfloat16 [16384, 8192], P(('ctx', 'head'), 'smp'), may hold values from -0.046875 to 0.046875
Outputs:
- mixed: bfloat16 [512, 8192], P(('group', 'ctx', 'head'), 'smp'), parts along dimension 0
There are 2 independent parts, one for each index of `group`. A program takes and returns all parts, laid end to end along the dimension named above; an argument that names none is the same for every part. Nothing has to cross between parts.
Inputs may be any that keep to these rules, and one draw needn't show every extreme that they name: `suffix_length`: the longest is exactly 128 in every draw. A permutation; cache row r and sample cache_sample[r] lie in the same group, the group of row r being (r // 32) % (2) and that of sample i being i // 128.
All inputs are finite; a program needn't handle non-finite values.
Results may differ from a plain program's by a relative error of at most 0.012.
Values may be sent and summed in bfloat16 or wider, within the bound.
No kernel may reach another device: no remote copies, remote signals or barrier semaphores. Data moves between devices by JAX's collectives and lax.ppermute only.
A program may use at most 192 MiB of HBM per device.

v0:
```python
import functools

import jax
import jax.numpy as jnp
from jax import lax
from jax.experimental import pallas as pl
from jax.experimental.pallas import tpu as pltpu
from jax.sharding import PartitionSpec as P

D = 8192
QUERY_HEADS = 64
KEY_VALUE_HEADS = 8
HD = 128
EPSILON = 1e-05

BF16 = jnp.bfloat16
F32 = jnp.float32
VMEM_LIMIT = 48 * 1024 * 1024
STAT_ROWS = 32
PIECES = 1
LOG2E = 1.4426950408889634
LN2 = 0.6931471805599453


def params(limit=VMEM_LIMIT):
    return pltpu.CompilerParams(vmem_limit_bytes=limit)


def cost(us):
    return pl.CostEstimate(
        flops=int(us * 1.1e9), bytes_accessed=int(us * 3.6e6), transcendentals=0
    )


IN_PLACE = pl.BlockSpec(memory_space=pl.ANY)
WHOLE = pl.BlockSpec(memory_space=pltpu.VMEM)
SCALARS = pl.BlockSpec(memory_space=pltpu.SMEM)


def run(name, kernel, in_specs, args, after=(), limit=VMEM_LIMIT, **more):
    n, m = len(args), len(after)

    def body(*refs):
        return kernel(*refs[:n], *refs[n + m :])

    return pl.pallas_call(
        body,
        name=name,
        in_specs=list(in_specs) + [IN_PLACE] * m,
        compiler_params=params(limit),
        **{"cost_estimate": cost(0.2), **more},
    )(*args, *after)


def dot(a, b):
    return jnp.dot(a, b, preferred_element_type=F32)


def dot_nt(a, b):
    return lax.dot_general(a, b, (((1,), (1,)), ((), ())), preferred_element_type=F32)


def split3(x):
    hi = x.astype(BF16).astype(F32)
    mid = (x - hi).astype(BF16).astype(F32)
    low = (x - hi - mid).astype(BF16).astype(F32)
    return hi, mid, low


def shift(x, axis, size, k):
    return lax.ppermute(x, axis, [(i, (i + k) % size) for i in range(size)])


def attention_kernel(
    heads,
    groups,
    where_ref,
    sample_hbm,
    length_hbm,
    q_hbm,
    prefix_hbm,
    suffix_hbm,
    msg_ref,
    sample_ref,
    length_ref,
    q_ref,
    prefix_ref,
    suffix_ref,
    number_sems,
    sems,
):
    samples = q_ref.shape[0]
    rows, span = suffix_ref.shape[1:3]
    lanes_s = rows * heads
    scale2 = HD**-0.5 * LOG2E
    q_at = pl.ds(pl.multiple_of(where_ref[0] * (heads * HD), HD), heads * HD)
    kv_at = pl.ds(pl.multiple_of(where_ref[1] * HD, HD), HD)
    numbers = [
        pltpu.make_async_copy(sample_hbm, sample_ref, number_sems.at[0]),
        pltpu.make_async_copy(length_hbm, length_ref, number_sems.at[1]),
    ]
    early = [
        pltpu.make_async_copy(q_hbm.at[:, q_at], q_ref, sems.at[0]),
        pltpu.make_async_copy(prefix_hbm.at[0, :, kv_at], prefix_ref.at[0], sems.at[1]),
        pltpu.make_async_copy(prefix_hbm.at[1, :, kv_at], prefix_ref.at[1], sems.at[2]),
    ]
    late = []
    some = rows // groups
    for which in range(2):
        for g in range(groups):
            part = pl.ds(g * some, some)
            late.append(
                pltpu.make_async_copy(
                    suffix_hbm.at[which, part, :, kv_at],
                    suffix_ref.at[which, part],
                    sems.at[3 + which * groups + g],
                )
            )
    for copy in numbers + early + late:
        copy.start()

    for copy in numbers:
        copy.wait()
    column = lax.broadcasted_iota(jnp.int32, (lanes_s, 1), 0) // heads
    across = lax.broadcasted_iota(jnp.int32, (1, lanes_s), 1) // heads
    ids = jnp.zeros((lanes_s, 1), jnp.int32)
    lens = jnp.zeros((1, lanes_s), jnp.int32)
    for r in range(rows):
        sample = lax.rem(sample_ref[where_ref[2] + r], samples)
        ids = jnp.where(column == r, sample, ids)
        lens = jnp.where(across == r, length_ref[sample], lens)
    shape = (lanes_s, heads * samples)
    lane = lax.broadcasted_iota(jnp.int32, shape, 1)
    row = lax.broadcasted_iota(jnp.int32, shape, 0)
    wanted = ids + lax.rem(row, heads) * samples
    pick = jnp.where(lane == wanted, 1.0, 0.0).astype(BF16)

    early[0].wait()
    queries = jnp.concatenate(
        [q_ref[:, g * HD : (g + 1) * HD] for g in range(heads)], axis=0
    )
    early[1].wait()
    early[2].wait()
    keys = prefix_ref[0]
    values_t = prefix_ref[1].T
    pieces = []
    for g in range(heads):
        s = dot_nt(keys, queries[g * samples : (g + 1) * samples])
        high = jnp.max(s, axis=0, keepdims=True) * scale2
        weights = jnp.exp2(s * scale2 - high)
        total = jnp.sum(weights, axis=0, keepdims=True)
        pieces.append((high, total, dot(values_t, weights.astype(BF16))))

    for copy in late:
        copy.wait()
    row_queries = dot(pick, queries)
    per_tile = min(rows, max(1, 128 // heads))
    width = per_tile * heads
    outs, lses = [], []
    for tile in range(rows // per_tile):
        at = tile * per_tile
        q_tile = row_queries[at * heads : at * heads + width]
        own = lax.broadcasted_iota(jnp.int32, (width, HD), 0) // heads
        q_wide = jnp.concatenate(
            [jnp.where(own == r, q_tile, 0.0).astype(BF16) for r in range(per_tile)], axis=1
        )
        row_keys = jnp.concatenate(
            [suffix_ref[0, at + r] for r in range(per_tile)], axis=1
        )
        s = dot_nt(row_keys, q_wide) * scale2
        t = lax.broadcasted_iota(jnp.int32, s.shape, 0)
        s = jnp.where(t < lens[:, at * heads : at * heads + width], s, -jnp.inf)
        high = jnp.max(s, axis=0, keepdims=True)
        weights = jnp.exp2(s - high)
        total = jnp.sum(weights, axis=0, keepdims=True)
        turned = weights.T
        own_t = lax.broadcasted_iota(jnp.int32, (width, span), 0) // heads
        w_wide = jnp.concatenate(
            [jnp.where(own_t == r, turned, 0.0).astype(BF16) for r in range(per_tile)], axis=1
        )
        values = suffix_ref[1, at : at + per_tile].reshape(per_tile * span, HD)
        outs.append(dot(w_wide, values).T / total)
        lses.append(high + jnp.log2(total))
    hi, mid, low = split3(jnp.concatenate(lses, axis=1))
    sub = lax.broadcasted_iota(jnp.int32, (16, lanes_s), 0)
    stats = jnp.where(sub == 0, hi, jnp.where(sub == 1, mid, jnp.where(sub == 2, low, 1.0)))
    to_place = jnp.concatenate([jnp.concatenate(outs, axis=1), stats], axis=0).astype(BF16)
    placed = dot(to_place, pick)
    placed_lse = placed[HD : HD + 1] + placed[HD + 1 : HD + 2] + placed[HD + 2 : HD + 3]
    present = placed[HD + 3 : HD + 4]

    rows_out = []
    for g, (high, total, out) in enumerate(pieces):
        at = slice(g * samples, (g + 1) * samples)
        here = present[:, at] > 0.5
        other = jnp.where(here, placed_lse[:, at], high)
        top = jnp.maximum(high, other)
        own_weight = jnp.exp2(high - top)
        other_weight = jnp.where(here, jnp.exp2(other - top), 0.0)
        both = own_weight * total + other_weight
        out = out * (own_weight / both) + placed[:HD, at] * (other_weight / both)
        msg_ref[g * HD : (g + 1) * HD, :] = out.astype(BF16)
        rows_out.append(top + jnp.log2(both))
    sub = lax.broadcasted_iota(jnp.int32, (STAT_ROWS, samples), 0)
    stats = jnp.zeros((STAT_ROWS, samples), F32)
    for g in range(heads):
        for part, value in enumerate(split3(rows_out[g])):
            stats = jnp.where(sub == part * heads + g, value, stats)
    msg_ref[heads * HD :, :] = stats.astype(BF16)


def attention_piece(where, cache_sample, suffix_length, queries, prefix, suffix, heads):
    samples = queries.shape[0]
    block, rows, span = prefix.shape[1], suffix.shape[1], suffix.shape[2]
    groups = 4 if rows % 4 == 0 else 1
    return run(
        "attention",
        functools.partial(attention_kernel, heads, groups),
        [SCALARS] + [IN_PLACE] * 5,
        [where, cache_sample, suffix_length, queries, prefix, suffix],
        out_specs=WHOLE,
        out_shape=jax.ShapeDtypeStruct((heads * HD + STAT_ROWS, samples), BF16),
        scratch_shapes=[
            pltpu.SMEM(cache_sample.shape, jnp.int32),
            pltpu.SMEM(suffix_length.shape, jnp.int32),
            pltpu.VMEM((samples, heads * HD), BF16),
            pltpu.VMEM((2, block, HD), BF16),
            pltpu.VMEM((2, rows, span, HD), BF16),
            pltpu.SemaphoreType.DMA((2,)),
            pltpu.SemaphoreType.DMA((3 + 2 * groups,)),
        ],
        cost_estimate=cost(5),
        limit=60 * 1024 * 1024,
    )


def merge_kernel(heads, *refs):
    pieces, out_ref = refs[:-1], refs[-1]
    top_rows = heads * HD
    lses = []
    for ref in pieces:
        stats = ref[top_rows:, :].astype(F32)
        lses.append(
            stats[:heads] + stats[heads : 2 * heads] + stats[2 * heads : 3 * heads]
        )
    top = functools.reduce(jnp.maximum, lses)
    weights = [jnp.exp2(lse - top) for lse in lses]
    denom = functools.reduce(jnp.add, weights)
    weights = [w / denom for w in weights]
    for g in range(heads):
        total = None
        for ref, w in zip(pieces, weights):
            term = ref[g * HD : (g + 1) * HD, :].astype(F32) * w[g : g + 1]
            total = term if total is None else total + term
        out_ref[:, g * HD : (g + 1) * HD] = total.T.astype(BF16)


def merge(pieces, heads):
    samples = pieces[0].shape[1]
    return run(
        "merge",
        functools.partial(merge_kernel, heads),
        [WHOLE] * len(pieces),
        pieces,
        out_specs=WHOLE,
        out_shape=jax.ShapeDtypeStruct((samples, heads * HD), BF16),
        cost_estimate=cost(1.3),
    )


def proj_kernel(n_ctx, n_head, own_rows, n_smp, parts, chunks, where_ref, *refs):
    attn_refs, w_hbm, refs = refs[:n_smp], refs[n_smp], refs[n_smp + 1 :]
    out_refs, (full, lhs, w_buf, sems) = refs[:-4], refs[-4:]
    ctx, smp, head = where_ref[0], where_ref[1], where_ref[2]
    samples = attn_refs[0].shape[0]
    tile = w_buf.shape[2]
    copies = [
        pltpu.make_async_copy(
            w_hbm.at[0, :, pl.ds(i * tile, tile)], w_buf.at[i], sems.at[i]
        )
        for i in range(chunks)
    ]
    for copy in copies:
        copy.start()
    for k, ref in enumerate(attn_refs):
        at = lax.rem(smp + n_smp - k, n_smp) * samples
        full[pl.ds(pl.multiple_of(at, 16), samples), :] = ref[...]
    step = own_rows // parts
    to = 0
    for b in range(n_head):
        h = lax.rem(head + b, n_head)
        for p in range(parts):
            for t in range(n_ctx):
                c = lax.rem(ctx + n_ctx - t, n_ctx)
                at = (c * n_head + h) * own_rows + p * step
                lhs[to : to + step, :] = full[pl.ds(pl.multiple_of(at, step), step), :]
                to += step
    for i, copy in enumerate(copies):
        copy.wait()
        out = dot(lhs[...], w_buf[i]).astype(BF16)
        row = 0
        for ref in out_refs:
            ref[:, i * tile : (i + 1) * tile] = out[row : row + ref.shape[0]]
            row += ref.shape[0]


def project(where, attn, w_out, n_ctx, n_head, own_rows, parts):
    n_smp = len(attn)
    samples, depth = attn[0].shape
    width = w_out.shape[2]
    chunks = 4
    tile = width // chunks
    per = n_ctx * own_rows // parts
    rows = per * parts * n_head
    return run(
        "project",
        functools.partial(proj_kernel, n_ctx, n_head, own_rows, n_smp, parts, chunks),
        [SCALARS] + [WHOLE] * n_smp + [IN_PLACE],
        [where, *attn, w_out],
        out_specs=[WHOLE] * (parts + n_head - 1),
        out_shape=[jax.ShapeDtypeStruct((per, width), BF16)] * parts
        + [jax.ShapeDtypeStruct((per * parts, width), BF16)] * (n_head - 1),
        scratch_shapes=[
            pltpu.VMEM((n_smp * samples, depth), BF16),
            pltpu.VMEM((rows, depth), BF16),
            pltpu.VMEM((chunks, depth, tile), BF16),
            pltpu.SemaphoreType.DMA((chunks,)),
        ],
        cost_estimate=cost(5),
    )


def add_heads_kernel(n_ctx, row, keep_ref, *refs):
    recv, outs = refs[:-n_ctx], refs[-n_ctx:]
    rows, width = outs[0].shape[0], recv[0].shape[1]
    pieces = outs[0].shape[1] // width
    for t, ref in enumerate(outs):
        for j in range(pieces):
            columns = slice(j * width, (j + 1) * width)
            total = keep_ref[t * rows : (t + 1) * rows, columns].astype(F32)
            for other in recv[j::pieces]:
                at = row + t * rows
                total = total + other[at : at + rows].astype(F32)
            ref[:, columns] = total.astype(BF16)


def send_heads(sends, pieces):
    step = sends[0].shape[1] // pieces
    return [
        shift(send[:, j * step : (j + 1) * step], "head", len(sends) + 1, b)
        for b, send in enumerate(sends, 1)
        for j in range(pieces)
    ]


def add_heads(keep, recv, row, n_ctx, after=()):
    rows, width = keep.shape
    return run(
        "add_heads",
        functools.partial(add_heads_kernel, n_ctx, row),
        [WHOLE] * (1 + len(recv)),
        [keep, *recv],
        after,
        out_specs=[WHOLE] * n_ctx,
        out_shape=[jax.ShapeDtypeStruct((rows // n_ctx, width), BF16)] * n_ctx,
    )


def far_first(n):
    return sorted(range(1, n), key=lambda k: -min(k, n - k))


def send_sums(sums):
    n_ctx = len(sums)
    return [sums[0]] + [shift(sums[t], "ctx", n_ctx, -t) for t in far_first(n_ctx)]


def send_rows(x, n_ctx):
    got = {t: shift(x, "ctx", n_ctx, t) for t in far_first(n_ctx)}
    return [x] + [got[t] for t in range(1, n_ctx)]


def join_kernel(*refs):
    pieces, out_ref = refs[:-1], refs[-1]
    rows = pieces[0].shape[0]
    for t, ref in enumerate(pieces):
        out_ref[t * rows : (t + 1) * rows, :] = ref[...]


def join(pieces, after):
    rows, width = pieces[0].shape
    return run(
        "join",
        join_kernel,
        [WHOLE] * len(pieces),
        pieces,
        after,
        out_specs=WHOLE,
        out_shape=jax.ShapeDtypeStruct((rows * len(pieces), width), BF16),
    )


def state_kernel(n_pieces, *refs):
    pieces, (res_ref, gain_ref, state_ref, msg_ref) = refs[:n_pieces], refs[n_pieces:]
    width = res_ref.shape[1]
    total = res_ref[...].astype(F32)
    for ref in pieces:
        total = total + ref[...].astype(F32)
    state = total.astype(BF16)
    state_ref[...] = state
    wide = state.astype(F32)
    msg_ref[:, :width] = (wide * gain_ref[...]).astype(BF16)
    hi, mid, low = split3(jnp.sum(wide * wide, axis=1, keepdims=True))
    lane = lax.broadcasted_iota(jnp.int32, (hi.shape[0], HD), 1)
    stats = jnp.where(
        lane == 0, hi, jnp.where(lane == 1, mid, jnp.where(lane == 2, low, 0.0))
    )
    msg_ref[:, width:] = stats.astype(BF16)


def make_state(pieces, residual, gain, after):
    rows, width = residual.shape
    return run(
        "state",
        functools.partial(state_kernel, len(pieces)),
        [WHOLE] * (len(pieces) + 2),
        [*pieces, residual, gain],
        after,
        out_specs=[WHOLE] * 2,
        out_shape=[
            jax.ShapeDtypeStruct((rows, width), BF16),
            jax.ShapeDtypeStruct((rows, width + HD), BF16),
        ],
    )


def finish_kernel(*refs):
    total = refs[0][...].astype(F32)
    for ref in refs[1:-1]:
        total = total + ref[...].astype(F32)
    refs[-1][...] = total.astype(refs[-1].dtype)


def finish(pieces):
    total = pieces[-1]
    for i in reversed(range(len(pieces) - 1)):
        total = run(
            "finish",
            finish_kernel,
            [WHOLE] * 2,
            [total, pieces[i]],
            out_specs=WHOLE,
            out_shape=jax.ShapeDtypeStruct(total.shape, F32 if i else BF16),
        )
    return total


def gate_up_kernel(chunks, n_parts, where_ref, *refs):
    parts, (g_hbm, u_hbm, out_ref, x, acc, g_buf, u_buf, g_sem, u_sem) = (
        refs[:n_parts],
        refs[n_parts:],
    )
    tile, units = g_buf.shape[1:]
    at = pl.multiple_of(where_ref[0] * units, 128)

    def chunk_copy(i, which):
        hbm, buf, sem = ((g_hbm, g_buf, g_sem), (u_hbm, u_buf, u_sem))[which]
        from_at = pl.multiple_of(i * tile, tile)
        return pltpu.make_async_copy(
            hbm.at[pl.ds(from_at, tile), pl.ds(at, units)], buf.at[i], sem.at[i]
        )

    for i in range(chunks):
        chunk_copy(i, 0).start()
        chunk_copy(i, 1).start()
    row = 0
    for ref in parts:
        x[row : row + ref.shape[0]] = ref[:, : x.shape[1]]
        row += ref.shape[0]
    acc[...] = jnp.zeros_like(acc)
    turns = 2

    @pl.loop(0, turns)
    def _(turn):
        gate = up = None
        for j in range(chunks // turns):
            i = turn * (chunks // turns) + j
            lhs = x[:, pl.ds(pl.multiple_of(i * tile, tile), tile)]
            chunk_copy(i, 0).wait()
            term = dot(lhs, g_buf[i])
            gate = term if gate is None else gate + term
            chunk_copy(i, 1).wait()
            term = dot(lhs, u_buf[i])
            up = term if up is None else up + term
        acc[:, :units] += gate
        acc[:, units:] += up

    out_ref[:, : 2 * units] = acc[...].astype(out_ref.dtype)
    row = 0
    for ref in parts:
        out_ref[row : row + ref.shape[0], 2 * units :] = ref[:, x.shape[1] :].astype(
            out_ref.dtype
        )
        row += ref.shape[0]


def gate_up(block, parts, gate_matrix, w_up, units, dtype, after=()):
    rows, depth = sum(p.shape[0] for p in parts), gate_matrix.shape[0]
    chunks = 8
    tile = depth // chunks
    return run(
        "gate_up",
        functools.partial(gate_up_kernel, chunks, len(parts)),
        [SCALARS] + [WHOLE] * len(parts) + [IN_PLACE] * 2,
        [block.reshape(1), *parts, gate_matrix, w_up],
        after,
        out_specs=WHOLE,
        out_shape=jax.ShapeDtypeStruct((rows, 2 * units + HD), dtype),
        scratch_shapes=[pltpu.VMEM((rows, depth), BF16), pltpu.VMEM((rows, 2 * units), F32)]
        + [pltpu.VMEM((chunks, tile, units), BF16)] * 2
        + [pltpu.SemaphoreType.DMA((chunks,))] * 2,
        cost_estimate=cost(2 + 4.2 * units / 1024),
    )


def act_kernel(own_ref, *refs):
    recv, out_ref = refs[:-1], refs[-1]
    total = own_ref[...]
    for ref in recv:
        total = total + ref[...].astype(F32)
    units = out_ref.shape[1]
    square = jnp.sum(total[:, 2 * units :], axis=1, keepdims=True)
    factor = lax.rsqrt(square / D + EPSILON)
    gate = factor * total[:, :units]
    up = factor * total[:, units : 2 * units]
    out_ref[...] = (gate / (1.0 + jnp.exp(-gate)) * up).astype(BF16)


def activate(own, recv, units, after):
    return run(
        "activate",
        act_kernel,
        [WHOLE] * (1 + len(recv)),
        [own, *recv],
        after,
        out_specs=WHOLE,
        out_shape=jax.ShapeDtypeStruct((own.shape[0], units), BF16),
    )


def down_kernel(n_parts, chunks, has_acc, last, n_head, where_ref, *refs):
    xs, refs = refs[:n_parts], refs[n_parts:]
    if has_acc:
        acc_ref, w_hbm, *outs, w_buf, sems = refs
    else:
        w_hbm, *outs, w_buf, sems = refs
    units, tile = w_buf.shape[2:]
    copies = []
    for i in range(chunks):
        for p in range(n_parts):
            at = pl.multiple_of(where_ref[p] * units, 16)
            copies.append(
                pltpu.make_async_copy(
                    w_hbm.at[pl.ds(at, units), pl.ds(i * tile, tile)],
                    w_buf.at[i, p],
                    sems.at[i, p],
                )
            )
    for copy in copies:
        copy.start()
    for i in range(chunks):
        total = acc_ref[:, i * tile : (i + 1) * tile] if has_acc else None
        for p in range(n_parts):
            copies[i * n_parts + p].wait()
            term = dot(xs[p][...], w_buf[i, p])
            total = term if total is None else total + term
        if last:
            per = total.shape[0] // n_head
            for b in range(n_head):
                outs[b][:, i * tile : (i + 1) * tile] = total[
                    b * per : (b + 1) * per
                ].astype(BF16)
        else:
            outs[0][:, i * tile : (i + 1) * tile] = total


def down(blocks, xs, w_down, acc, last, n_head, after):
    rows, units = xs[0].shape
    width = w_down.shape[1]
    chunks = 4
    tile = width // chunks
    n = len(xs)
    args = list(xs) + ([] if acc is None else [acc])
    if last:
        out_shape = [jax.ShapeDtypeStruct((rows // n_head, width), BF16)] * n_head
    else:
        out_shape = [jax.ShapeDtypeStruct((rows, width), F32)]
    out = run(
        "down",
        functools.partial(down_kernel, n, chunks, acc is not None, last, n_head),
        [SCALARS] + [WHOLE] * len(args) + [IN_PLACE],
        [jnp.stack(blocks), *args, w_down],
        after,
        out_specs=[WHOLE] * len(out_shape),
        out_shape=out_shape,
        scratch_shapes=[
            pltpu.VMEM((chunks, n, units, tile), BF16),
            pltpu.SemaphoreType.DMA((chunks, n)),
        ],
        cost_estimate=cost(4 * n),
    )
    return out if last else out[0]


def on_device(
    n_ctx,
    n_smp,
    n_head,
    queries,
    prefix_cache,
    suffix_cache,
    suffix_length,
    cache_sample,
    residual,
    w_out,
    norm_gain,
    gate_matrix,
    w_up,
    w_down,
):
    ctx, smp, head = (lax.axis_index(name) for name in ("ctx", "smp", "head"))
    samples = queries.shape[0]
    own_rows = residual.shape[0]
    queries = queries.reshape(samples, -1)
    prefix = prefix_cache.reshape(2, prefix_cache.shape[1], -1)
    rows, span = suffix_cache.shape[1:3]
    suffix = suffix_cache.reshape(2, rows, span, -1)
    kv_heads = prefix.shape[2] // HD
    group = QUERY_HEADS // KEY_VALUE_HEADS
    heads = kv_heads * group // n_ctx

    base = (ctx * n_smp + smp) * rows
    pieces = []
    for k in far_first(n_ctx) + [0]:
        chunk = (ctx + k) % n_ctx
        kv = chunk * heads // group
        at = jnp.stack([chunk, kv, base])
        piece = attention_piece(
            at, cache_sample, suffix_length, queries, prefix, suffix, heads
        )
        pieces.append(shift(piece, "ctx", n_ctx, k) if k else piece)

    parts = 2 if own_rows % 32 == 0 else 1
    step = own_rows // parts
    where = jnp.stack([ctx, smp, head])
    every = range(parts)
    others = range(1, n_smp)
    attn = merge(pieces, heads)
    gathered = [attn] + [shift(attn, "smp", n_smp, k) for k in others]
    by_head = project(where, gathered, w_out, n_ctx, n_head, own_rows, parts)
    recv = send_heads(by_head[parts:], 1)
    all_sums = [
        add_heads(by_head[p], recv, p * by_head[p].shape[0], n_ctx) for p in every
    ]
    units = gate_matrix.shape[1] // n_smp
    states, rows, full = [None] * parts, [None] * parts, [None] * parts
    received, own, hidden, theirs = ([None] * parts for _ in range(4))
    sums = [None] * parts
    done = []

    def state_step(p):
        nonlocal done
        states[p], message = make_state(
            send_sums(all_sums[p]), residual[p * step : (p + 1) * step], gain, done
        )
        rows[p] = send_rows(message, n_ctx)
        done = [states[p]]

    def others_step(p):
        nonlocal done
        joined = join(rows[p], done)
        full[p] = [shift(joined, "head", n_head, b) if b else joined for b in range(n_head)]
        received[p] = []
        for k in others:
            block = (smp + k) % n_smp
            send = gate_up(block, full[p], gate_matrix, w_up, units, BF16, done)
            done = [send]
            received[p].append(shift(send, "smp", n_smp, k))

    def own_step(p):
        nonlocal done
        own[p] = gate_up(smp, full[p], gate_matrix, w_up, units, F32, done)
        done = [own[p]]

    def hidden_step(p):
        nonlocal done
        hidden[p] = activate(own[p], received[p], units, done)
        theirs[p] = [shift(hidden[p], "smp", n_smp, k) for k in others]
        done = [hidden[p]]

    blocks = [(smp + n_smp - k) % n_smp for k in range(n_smp)]

    def down_step(p, first, count, acc):
        nonlocal done
        xs = [hidden[p], *theirs[p]][first : first + count]
        last = first + count == n_smp
        out = down(blocks[first : first + count], xs, w_down, acc, last, n_head, done)
        done = [out[0] if last else out]
        return out

    gain = norm_gain[None, :]
    state_step(0)
    for p in every:
        others_step(p)
        if p + 1 < parts:
            state_step(p + 1)
            own_step(p)
            hidden_step(p)
            continue
        own_step(p)
        for q in range(p):
            keep, *sends = down_step(q, 0, n_smp, None)
            sums[q] = add_heads(keep, send_heads(sends, 1), 0, n_ctx)
        hidden_step(p)
        acc = down_step(p, 0, 1, None)
        outs = [finish([states[q], *send_sums(sums[q])]) for q in range(p)]
        done = done + outs
        keep, *sends = down_step(p, 1, n_smp - 1, acc)
    sums[-1] = add_heads(keep, send_heads(sends, PIECES), 0, n_ctx)
    outs.append(finish([states[-1], *send_sums(sums[-1])]))
    return jnp.concatenate(outs, axis=0)


def solution(mesh):
    in_specs = (
        P(("group", "smp"), "head", None),
        P(None, ("group", "ctx"), "head", None),
        P(None, ("group", "ctx", "smp"), None, "head", None),
        P(("group", "smp")),
        P("group"),
        P(("group", "ctx", "head"), "smp"),
        P("head", "ctx", "smp"),
        P("smp"),
        P("smp", ("ctx", "head")),
        P("smp", ("ctx", "head")),
        P(("ctx", "head"), "smp"),
    )
    out_specs = P(("group", "ctx", "head"), "smp")
    body = functools.partial(
        on_device, mesh.shape["ctx"], mesh.shape["smp"], mesh.shape["head"]
    )
    return jax.shard_map(
        body, mesh=mesh, in_specs=in_specs, out_specs=out_specs, check_vma=False
    )
```

profile of v0, /device:TPU:0, one launch (start us, length us, event | category | flops | bytes accessed | tf_op | source)
XLA Modules:
  0.0 174.5 jit_solution(11091652628286243948)
XLA Ops:
  0.6 6.5 %attention.4 = bf16[1056,128]{1,0:T(8,128)(2,1)} custom-call(s32[3]{0:T(128)} %add_add_fusion.refs_0_, s32[256]{0:T(256)} %refs_1_.7, s32[128]{0:T(128)} %refs_2_.8, bf16[128,4096]{1,0:T(8,128)(2,1)} %bitcast.28, bf16[2,1024,512]{2,1,0:T(8,128)(2,1)} %bitcast.24, bf16[2,32,128,512]{3,2,1,0:T(8,128)(2,1)} %bitcast.20), custom_call_target="tpu_custom_call" | custom-call | flops 5500000256 | bytes 18000000 | tf_op jit(solution)/shard_map/attention/pallas_call | solution.py:46
  7.1 4.1 %collective-permute-start = (bf16[1056,128]{1,0:T(8,128)(2,1)}, bf16[1056,128]{1,0:T(8,128)(2,1)S(1)}, u32[]{:S(2)}, u32[]{:S(2)}) collective-permute-start(bf16[1056,128]{1,0:T(8,128)(2,1)} %attention.4), channel_id=1, source_target_pairs={{0,8},{4,12},{8,0},{12,4},{1,9},{5,13},{9,1},{13,5},{2,10},{6,14},... | collective-permute-start | bytes 811016 | tf_op jit(solution)/shard_map/ppermute | solution.py:71
  11.8 6.5 %attention.5 = bf16[1056,128]{1,0:T(8,128)(2,1)} custom-call(s32[3]{0:T(128)} %add_add_fusion.1.refs_0_, s32[256]{0:T(256)} %refs_1_.7, s32[128]{0:T(128)} %refs_2_.8, bf16[128,4096]{1,0:T(8,128)(2,1)} %bitcast.29, bf16[2,1024,512]{2,1,0:T(8,128)(2,1)} %bitcast.25, bf16[2,32,128,512]{3,2,1,0:T(8,128)(2,1)} %bitcast.21), custom_call_target="tpu_custom_call" | custom-call | flops 5500000256 | bytes 18000000 | tf_op jit(solution)/shard_map/attention/pallas_call | solution.py:46
  20.5 6.5 %attention.6 = bf16[1056,128]{1,0:T(8,128)(2,1)} custom-call(s32[3]{0:T(128)} %add_add_fusion.2.refs_0_, s32[256]{0:T(256)} %refs_1_.7, s32[128]{0:T(128)} %refs_2_.8, bf16[128,4096]{1,0:T(8,128)(2,1)} %bitcast.30, bf16[2,1024,512]{2,1,0:T(8,128)(2,1)} %bitcast.26, bf16[2,32,128,512]{3,2,1,0:T(8,128)(2,1)} %bitcast.22), custom_call_target="tpu_custom_call" | custom-call | flops 5500000256 | bytes 18000000 | tf_op jit(solution)/shard_map/attention/pallas_call | solution.py:46
  30.1 6.5 %attention.7.refs_3_ = bf16[1056,128]{1,0:T(8,128)(2,1)} custom-call(s32[3]{0:T(128)} %add_add_fusion.3.refs_0_, s32[256]{0:T(256)} %refs_1_.7, s32[128]{0:T(128)} %refs_2_.8, bf16[128,4096]{1,0:T(8,128)(2,1)} %bitcast.31, bf16[2,1024,512]{2,1,0:T(8,128)(2,1)} %bitcast.27, bf16[2,32,128,512]{3,2,1,0:T(8,128)(2,1)} %bitcast.23), custom_call_target="tpu_custom_call" | custom-call | flops 5500000256 | bytes 18000000 | tf_op jit(solution)/shard_map/attention/pallas_call | solution.py:46
  39.5 5.6 %collective-permute-done.3.refs_2_ = bf16[128,1024]{1,0:T(8,128)(2,1)S(1)} collective-permute-done((bf16[128,1024]{1,0:T(8,128)(2,1)S(1)}, bf16[128,1024]{1,0:T(8,128)(2,1)S(1)}, u32[]{:S(2)}, u32[]{:S(2)}) %collective-permute-start.3) | collective-permute-done | bytes 262176 | tf_op jit(solution)/shard_map/ppermute | solution.py:71
  45.2 5.0 %project.1 = (bf16[64,4096]{1,0:T(8,128)(2,1)S(1)}, bf16[64,4096]{1,0:T(8,128)(2,1)S(1)}, bf16[128,4096]{1,0:T(8,128)(2,1)S(1)}) custom-call(s32[3]{0:T(128)S(1)} %pad_add_fusion.1.refs_0_, bf16[128,1024]{1,0:T(8,128)(2,1)S(1)} %merge.1.refs_1_, bf16[128,1024]{1,0:T(8,128)(2,1)S(1)} %collective-permute-done.3.refs_2_, bf16[1,1024,4096]{2,1,0:T(8,128)(2,1)} %refs_3_.7), custom_call_target="tpu_custom_call" | custom-call | flops 5500000256 | bytes 18000000 | tf_op jit(solution)/shard_map/project/pallas_call | solution.py:46
  55.6 9.0 %collective-permute-done.5.refs_1_ = bf16[16,4096]{1,0:T(8,128)(2,1)S(1)} collective-permute-done((bf16[16,4096]{1,0:T(8,128)(2,1)S(1)}, bf16[16,4096]{1,0:T(8,128)(2,1)S(1)}, u32[]{:S(2)}, u32[]{:S(2)}) %collective-permute-start.5) | collective-permute-done | bytes 131104 | tf_op jit(solution)/shard_map/ppermute | solution.py:71
  64.9 3.3 %collective-permute-start.10 = (bf16[16,4224]{1,0:T(8,128)(2,1)S(1)}, bf16[16,4224]{1,0:T(8,128)(2,1)S(1)}, u32[]{:S(2)}, u32[]{:S(2)}) collective-permute-start(bf16[16,4224]{1,0:T(8,128)(2,1)S(1)} %get-tuple-element.38.refs_0_), channel_id=1, source_target_pairs={{0,12},{4,0},{8,4},{12,8},{1,13},{5,1},{9,5},{13,9},{2,14},{6,2},{... | collective-permute-start | bytes 405512 | tf_op jit(solution)/shard_map/ppermute | solution.py:71
  72.2 9.5 %collective-permute-done.9.refs_2_ = bf16[16,4224]{1,0:T(8,128)(2,1)S(1)} collective-permute-done((bf16[16,4224]{1,0:T(8,128)(2,1)S(1)}, bf16[16,4224]{1,0:T(8,128)(2,1)S(1)}, u32[]{:S(2)}, u32[]{:S(2)}) %collective-permute-start.9) | collective-permute-done | bytes 135200 | tf_op jit(solution)/shard_map/ppermute | solution.py:71
  84.8 6.4 %gate_up.4.refs_6_ = bf16[128,2176]{1,0:T(8,128)(2,1)S(1)} custom-call(s32[1]{0:T(128)} %bitcast.1.refs_0_, bf16[64,4224]{1,0:T(8,128)(2,1)S(1)} %join.2.refs_1_, bf16[64,4224]{1,0:T(8,128)(2,1)S(1)} %collective-permute-done.11.refs_2_, bf16[4096,2048]{1,0:T(8,128)(2,1)} %refs_3_.11, bf16[4096,2048]{1,0:T(8,128)(2,1)} %refs_4_.7, ...), custom_call_target="tpu_custom_call" | custom-call | flops 6819999744 | bytes 22320000 | tf_op jit(solution)/shard_map/gate_up/pallas_call | solution.py:46
  91.2 2.8 %collective-permute-done.13.refs_2_ = bf16[16,4096]{1,0:T(8,128)(2,1)S(1)} collective-permute-done((bf16[16,4096]{1,0:T(8,128)(2,1)S(1)}, bf16[16,4096]{1,0:T(8,128)(2,1)S(1)}, u32[]{:S(2)}, u32[]{:S(2)}) %collective-permute-start.13) | collective-permute-done | bytes 131104 | tf_op jit(solution)/shard_map/ppermute | solution.py:71
  99.4 6.4 %gate_up.5.refs_0_.refs_2_ = f32[128,2176]{1,0:T(8,128)S(1)} custom-call(s32[1]{0:T(128)} %bitcast.2.refs_0_, bf16[64,4224]{1,0:T(8,128)(2,1)S(1)} %join.2.refs_1_, bf16[64,4224]{1,0:T(8,128)(2,1)S(1)} %collective-permute-done.11.refs_2_, bf16[4096,2048]{1,0:T(8,128)(2,1)} %refs_3_.11, bf16[4096,2048]{1,0:T(8,128)(2,1)} %refs_4_.7, ...), custom_call_target="tpu_custom_call" | custom-call | flops 6819999744 | bytes 22320000 | tf_op jit(solution)/shard_map/gate_up/pallas_call | solution.py:46
  105.7 6.1 %collective-permute-done.15.refs_1_ = bf16[128,2176]{1,0:T(8,128)(2,1)S(1)} collective-permute-done((bf16[128,2176]{1,0:T(8,128)(2,1)S(1)}, bf16[128,2176]{1,0:T(8,128)(2,1)S(1)}, u32[]{:S(2)}, u32[]{:S(2)}) %collective-permute-start.15) | collective-permute-done | bytes 557088 | tf_op jit(solution)/shard_map/ppermute | solution.py:71
  114.3 6.3 %gate_up.6.refs_5_ = bf16[128,2176]{1,0:T(8,128)(2,1)S(1)} custom-call(s32[1]{0:T(128)} %bitcast.1.refs_0_, bf16[64,4224]{1,0:T(8,128)(2,1)S(1)} %join.3.refs_1_, bf16[64,4224]{1,0:T(8,128)(2,1)S(1)} %collective-permute-done.20.refs_2_, bf16[4096,2048]{1,0:T(8,128)(2,1)} %refs_3_.11, bf16[4096,2048]{1,0:T(8,128)(2,1)} %refs_4_.7, ...), custom_call_target="tpu_custom_call" | custom-call | flops 6819999744 | bytes 22320000 | tf_op jit(solution)/shard_map/gate_up/pallas_call | solution.py:46
  122.2 6.4 %gate_up.7.refs_4_.refs_0_ = f32[128,2176]{1,0:T(8,128)S(1)} custom-call(s32[1]{0:T(128)} %bitcast.2.refs_0_, bf16[64,4224]{1,0:T(8,128)(2,1)S(1)} %join.3.refs_1_, bf16[64,4224]{1,0:T(8,128)(2,1)S(1)} %collective-permute-done.20.refs_2_, bf16[4096,2048]{1,0:T(8,128)(2,1)} %refs_3_.11, bf16[4096,2048]{1,0:T(8,128)(2,1)} %refs_4_.7, ...), custom_call_target="tpu_custom_call" | custom-call | flops 6819999744 | bytes 22320000 | tf_op jit(solution)/shard_map/gate_up/pallas_call | solution.py:46
  128.6 7.3 %down.3 = (bf16[64,4096]{1,0:T(8,128)(2,1)S(1)}, bf16[64,4096]{1,0:T(8,128)(2,1)S(1)}) custom-call(s32[2]{0:T(128)S(1)} %pad_add_fusion.refs_0_, bf16[128,1024]{1,0:T(8,128)(2,1)S(1)} %activate.2.refs_4_.refs_5_.refs_1_, bf16[128,1024]{1,0:T(8,128)(2,1)S(1)} %collective-permute-done.16.refs_2_, bf16[2048,4096]{1,0:T(8,128)(2,1)} %refs_3_.13, ...), custom_call_target="tpu_custom_call" | custom-call | flops 8800000000 | bytes 28800000 | tf_op jit(solution)/shard_map/down/pallas_call | solution.py:46
  138.6 3.3 %collective-permute-start.23 = (bf16[16,4096]{1,0:T(8,128)(2,1)S(1)}, bf16[16,4096]{1,0:T(8,128)(2,1)S(1)}, u32[]{:S(2)}, u32[]{:S(2)}) collective-permute-start(bf16[16,4096]{1,0:T(8,128)(2,1)S(1)} %get-tuple-element.50), channel_id=1, source_target_pairs={{0,12},{4,0},{8,4},{12,8},{1,13},{5,1},{9,5},{13,9},{2,14},{6,2},{... | collective-permute-start | bytes 393224 | tf_op jit(solution)/shard_map/ppermute | solution.py:71
  143.1 4.0 %down.4.refs_2_.refs_4_ = f32[128,4096]{1,0:T(8,128)S(1)} custom-call(s32[1]{0:T(128)} %bitcast.refs_0_, bf16[128,1024]{1,0:T(8,128)(2,1)S(1)} %activate.3.refs_1_.refs_3_, bf16[2048,4096]{1,0:T(8,128)(2,1)} %refs_3_.13, bf16[128,1024]{1,0:T(8,128)(2,1)S(1)} %activate.3.refs_1_.refs_3_), custom_call_target="tpu_custom_call" | custom-call | flops 4400000000 | bytes 14400000 | tf_op jit(solution)/shard_map/down/pallas_call | solution.py:46
  147.1 6.7 %collective-permute-done.24.refs_1_ = bf16[16,4096]{1,0:T(8,128)(2,1)S(1)} collective-permute-done((bf16[16,4096]{1,0:T(8,128)(2,1)S(1)}, bf16[16,4096]{1,0:T(8,128)(2,1)S(1)}, u32[]{:S(2)}, u32[]{:S(2)}) %collective-permute-start.24) | collective-permute-done | bytes 131104 | tf_op jit(solution)/shard_map/ppermute | solution.py:71
  153.9 4.0 %down.5 = (bf16[64,4096]{1,0:T(8,128)(2,1)S(1)}, bf16[64,4096]{1,0:T(8,128)(2,1)S(1)}) custom-call(s32[1]{0:T(128)} %bitcast.1.refs_0_, bf16[128,1024]{1,0:T(8,128)(2,1)S(1)} %collective-permute-done.26.refs_1_, f32[128,4096]{1,0:T(8,128)S(1)} %down.4.refs_2_.refs_4_, bf16[2048,4096]{1,0:T(8,128)(2,1)} %refs_3_.13, f32[128,4096]{1,0:T(8,128)S(1)} %down.4.refs_2_.refs_4_, ...), custom_call_target="tpu_custom_call" | custom-call | flops 4400000000 | bytes 14400000 | tf_op jit(solution)/shard_map/down/pallas_call | solution.py:46
  160.0 3.8 %collective-permute-start.29 = (bf16[16,4096]{1,0:T(8,128)(2,1)S(1)}, bf16[16,4096]{1,0:T(8,128)(2,1)S(1)}, u32[]{:S(2)}, u32[]{:S(2)}) collective-permute-start(bf16[16,4096]{1,0:T(8,128)(2,1)S(1)} %get-tuple-element.56), channel_id=1, source_target_pairs={{0,12},{4,0},{8,4},{12,8},{1,13},{5,1},{9,5},{13,9},{2,14},{6,2},{... | collective-permute-start | bytes 393224 | tf_op jit(solution)/shard_map/ppermute | solution.py:71
  163.9 4.4 %collective-permute-done.28.refs_0_ = bf16[16,4096]{1,0:T(8,128)(2,1)S(1)} collective-permute-done((bf16[16,4096]{1,0:T(8,128)(2,1)S(1)}, bf16[16,4096]{1,0:T(8,128)(2,1)S(1)}, u32[]{:S(2)}, u32[]{:S(2)}) %collective-permute-start.28) | collective-permute-done | bytes 131104 | tf_op jit(solution)/shard_map/ppermute | solution.py:71
  170.3 3.4 %collective-permute-done.30.refs_1_ = bf16[16,4096]{1,0:T(8,128)(2,1)S(1)} collective-permute-done((bf16[16,4096]{1,0:T(8,128)(2,1)S(1)}, bf16[16,4096]{1,0:T(8,128)(2,1)S(1)}, u32[]{:S(2)}, u32[]{:S(2)}) %collective-permute-start.30) | collective-permute-done | bytes 131104 | tf_op jit(solution)/shard_map/ppermute | solution.py:71
  (83 shorter events, 40.5 us)
Async XLA Ops:
  7.1 29.5 %collective-permute-start = (bf16[1056,128]{1,0:T(8,128)(2,1)}, bf16[1056,128]{1,0:T(8,128)(2,1)S(1)}, u32[]{:S(2)}, u32[]{:S(2)}) collective-permute-start(bf16[1056,128]{1,0:T(8,128)(2,1)} %attention.4), channel_id=1, source_target_pairs={{0,8},{4,12},{8,0},{12,4},{1,9},{5,13},{9,1},{13,5},{2,10},{6,14},... | collective-permute-start | bytes 811016 | tf_op jit(solution)/shard_map/ppermute | solution.py:71
  18.3 18.4 %collective-permute-start.1 = (bf16[1056,128]{1,0:T(8,128)(2,1)}, bf16[1056,128]{1,0:T(8,128)(2,1)S(1)}, u32[]{:S(2)}, u32[]{:S(2)}) collective-permute-start(bf16[1056,128]{1,0:T(8,128)(2,1)} %attention.5), channel_id=1, source_target_pairs={{0,4},{4,8},{8,12},{12,0},{1,5},{5,9},{9,13},{13,1},{2,6},{6,10},{... | collective-permute-start | bytes 811016 | tf_op jit(solution)/shard_map/ppermute | solution.py:71
  27.0 9.7 %collective-permute-start.2 = (bf16[1056,128]{1,0:T(8,128)(2,1)}, bf16[1056,128]{1,0:T(8,128)(2,1)S(1)}, u32[]{:S(2)}, u32[]{:S(2)}) collective-permute-start(bf16[1056,128]{1,0:T(8,128)(2,1)} %attention.6), channel_id=1, source_target_pairs={{0,12},{4,0},{8,4},{12,8},{1,13},{5,1},{9,5},{13,9},{2,14},{6,2},{... | collective-permute-start | bytes 811016 | tf_op jit(solution)/shard_map/ppermute | solution.py:71
  53.1 11.5 %collective-permute-start.5 = (bf16[16,4096]{1,0:T(8,128)(2,1)S(1)}, bf16[16,4096]{1,0:T(8,128)(2,1)S(1)}, u32[]{:S(2)}, u32[]{:S(2)}) collective-permute-start(bf16[16,4096]{1,0:T(8,128)(2,1)S(1)} %get-tuple-element.35), channel_id=1, source_target_pairs={{0,8},{4,12},{8,0},{12,4},{1,9},{5,13},{9,1},{13,5},{2,10},{6,14},... | collective-permute-start | bytes 393224 | tf_op jit(solution)/shard_map/ppermute | solution.py:71
  53.1 11.5 %collective-permute-start.6 = (bf16[16,4096]{1,0:T(8,128)(2,1)S(1)}, bf16[16,4096]{1,0:T(8,128)(2,1)S(1)}, u32[]{:S(2)}, u32[]{:S(2)}) collective-permute-start(bf16[16,4096]{1,0:T(8,128)(2,1)S(1)} %get-tuple-element.36), channel_id=1, source_target_pairs={{0,12},{4,0},{8,4},{12,8},{1,13},{5,1},{9,5},{13,9},{2,14},{6,2},{... | collective-permute-start | bytes 393224 | tf_op jit(solution)/shard_map/ppermute | solution.py:71
  55.3 9.4 %collective-permute-start.7 = (bf16[16,4096]{1,0:T(8,128)(2,1)S(1)}, bf16[16,4096]{1,0:T(8,128)(2,1)S(1)}, u32[]{:S(2)}, u32[]{:S(2)}) collective-permute-start(bf16[16,4096]{1,0:T(8,128)(2,1)S(1)} %get-tuple-element.37), channel_id=1, source_target_pairs={{0,4},{4,8},{8,12},{12,0},{1,5},{5,9},{9,13},{13,1},{2,6},{6,10},{... | collective-permute-start | bytes 393224 | tf_op jit(solution)/shard_map/ppermute | solution.py:71
  68.2 13.5 %collective-permute-start.9 = (bf16[16,4224]{1,0:T(8,128)(2,1)S(1)}, bf16[16,4224]{1,0:T(8,128)(2,1)S(1)}, u32[]{:S(2)}, u32[]{:S(2)}) collective-permute-start(bf16[16,4224]{1,0:T(8,128)(2,1)S(1)} %get-tuple-element.38.refs_0_), channel_id=1, source_target_pairs={{0,8},{4,12},{8,0},{12,4},{1,9},{5,13},{9,1},{13,5},{2,10},{6,14},... | collective-permute-start | bytes 405512 | tf_op jit(solution)/shard_map/ppermute | solution.py:71
  69.5 12.2 %collective-permute-start.8 = (bf16[16,4224]{1,0:T(8,128)(2,1)S(1)}, bf16[16,4224]{1,0:T(8,128)(2,1)S(1)}, u32[]{:S(2)}, u32[]{:S(2)}) collective-permute-start(bf16[16,4224]{1,0:T(8,128)(2,1)S(1)} %get-tuple-element.38.refs_0_), channel_id=1, source_target_pairs={{0,4},{4,8},{8,12},{12,0},{1,5},{5,9},{9,13},{13,1},{2,6},{6,10},{... | collective-permute-start | bytes 405512 | tf_op jit(solution)/shard_map/ppermute | solution.py:71
  81.9 9.3 %collective-permute-start.12 = (bf16[16,4096]{1,0:T(8,128)(2,1)S(1)}, bf16[16,4096]{1,0:T(8,128)(2,1)S(1)}, u32[]{:S(2)}, u32[]{:S(2)}) collective-permute-start(bf16[16,4096]{1,0:T(8,128)(2,1)S(1)} %get-tuple-element.42), channel_id=1, source_target_pairs={{0,8},{4,12},{8,0},{12,4},{1,9},{5,13},{9,1},{13,5},{2,10},{6,14},... | collective-permute-start | bytes 393224 | tf_op jit(solution)/shard_map/ppermute | solution.py:71
  82.8 11.2 %collective-permute-start.13 = (bf16[16,4096]{1,0:T(8,128)(2,1)S(1)}, bf16[16,4096]{1,0:T(8,128)(2,1)S(1)}, u32[]{:S(2)}, u32[]{:S(2)}) collective-permute-start(bf16[16,4096]{1,0:T(8,128)(2,1)S(1)} %get-tuple-element.43), channel_id=1, source_target_pairs={{0,12},{4,0},{8,4},{12,8},{1,13},{5,1},{9,5},{13,9},{2,14},{6,2},{... | collective-permute-start | bytes 393224 | tf_op jit(solution)/shard_map/ppermute | solution.py:71
  83.2 10.8 %collective-permute-start.14 = (bf16[16,4096]{1,0:T(8,128)(2,1)S(1)}, bf16[16,4096]{1,0:T(8,128)(2,1)S(1)}, u32[]{:S(2)}, u32[]{:S(2)}) collective-permute-start(bf16[16,4096]{1,0:T(8,128)(2,1)S(1)} %get-tuple-element.44), channel_id=1, source_target_pairs={{0,4},{4,8},{8,12},{12,0},{1,5},{5,9},{9,13},{13,1},{2,6},{6,10},{... | collective-permute-start | bytes 393224 | tf_op jit(solution)/shard_map/ppermute | solution.py:71
  94.2 18.0 %collective-permute-start.19 = (bf16[16,4224]{1,0:T(8,128)(2,1)S(1)}, bf16[16,4224]{1,0:T(8,128)(2,1)S(1)}, u32[]{:S(2)}, u32[]{:S(2)}) collective-permute-start(bf16[16,4224]{1,0:T(8,128)(2,1)S(1)} %get-tuple-element.46.refs_0_), channel_id=1, source_target_pairs={{0,12},{4,0},{8,4},{12,8},{1,13},{5,1},{9,5},{13,9},{2,14},{6,2},{... | collective-permute-start | bytes 405512 | tf_op jit(solution)/shard_map/ppermute | solution.py:71
  95.0 17.2 %collective-permute-start.18 = (bf16[16,4224]{1,0:T(8,128)(2,1)S(1)}, bf16[16,4224]{1,0:T(8,128)(2,1)S(1)}, u32[]{:S(2)}, u32[]{:S(2)}) collective-permute-start(bf16[16,4224]{1,0:T(8,128)(2,1)S(1)} %get-tuple-element.46.refs_0_), channel_id=1, source_target_pairs={{0,8},{4,12},{8,0},{12,4},{1,9},{5,13},{9,1},{13,5},{2,10},{6,14},... | collective-permute-start | bytes 405512 | tf_op jit(solution)/shard_map/ppermute | solution.py:71
  97.8 14.4 %collective-permute-start.17 = (bf16[16,4224]{1,0:T(8,128)(2,1)S(1)}, bf16[16,4224]{1,0:T(8,128)(2,1)S(1)}, u32[]{:S(2)}, u32[]{:S(2)}) collective-permute-start(bf16[16,4224]{1,0:T(8,128)(2,1)S(1)} %get-tuple-element.46.refs_0_), channel_id=1, source_target_pairs={{0,4},{4,8},{8,12},{12,0},{1,5},{5,9},{9,13},{13,1},{2,6},{6,10},{... | collective-permute-start | bytes 405512 | tf_op jit(solution)/shard_map/ppermute | solution.py:71
  97.9 14.0 %collective-permute-start.15 = (bf16[128,2176]{1,0:T(8,128)(2,1)S(1)}, bf16[128,2176]{1,0:T(8,128)(2,1)S(1)}, u32[]{:S(2)}, u32[]{:S(2)}) collective-permute-start(bf16[128,2176]{1,0:T(8,128)(2,1)S(1)} %gate_up.4.refs_6_), channel_id=1, source_target_pairs={{0,2},{2,0},{1,3},{3,1},{4,6},{6,4},{5,7},{7,5},{8,10},{10,8},{9,1... | collective-permute-start | bytes 1671176 | tf_op jit(solution)/shard_map/ppermute | solution.py:71
  112.4 16.1 %collective-permute-start.16 = (bf16[128,1024]{1,0:T(8,128)(2,1)S(1)}, bf16[128,1024]{1,0:T(8,128)(2,1)S(1)}, u32[]{:S(2)}, u32[]{:S(2)}) collective-permute-start(bf16[128,1024]{1,0:T(8,128)(2,1)S(1)} %activate.2.refs_4_.refs_5_.refs_1_), channel_id=1, source_target_pairs={{0,2},{2,0},{1,3},{3,1},{4,6},{6,4},{5,7},{7,5},{8,10},{10,8},{9,1... | collective-permute-start | bytes 786440 | tf_op jit(solution)/shard_map/ppermute | solution.py:71
  120.6 21.5 %collective-permute-start.25 = (bf16[128,2176]{1,0:T(8,128)(2,1)S(1)}, bf16[128,2176]{1,0:T(8,128)(2,1)S(1)}, u32[]{:S(2)}, u32[]{:S(2)}) collective-permute-start(bf16[128,2176]{1,0:T(8,128)(2,1)S(1)} %gate_up.6.refs_5_), channel_id=1, source_target_pairs={{0,2},{2,0},{1,3},{3,1},{4,6},{6,4},{5,7},{7,5},{8,10},{10,8},{9,1... | collective-permute-start | bytes 1671176 | tf_op jit(solution)/shard_map/ppermute | solution.py:71
  137.9 9.1 %collective-permute-start.22 = (bf16[16,4096]{1,0:T(8,128)(2,1)S(1)}, bf16[16,4096]{1,0:T(8,128)(2,1)S(1)}, u32[]{:S(2)}, u32[]{:S(2)}) collective-permute-start(bf16[16,4096]{1,0:T(8,128)(2,1)S(1)} %get-tuple-element.49), channel_id=1, source_target_pairs={{0,4},{4,8},{8,12},{12,0},{1,5},{5,9},{9,13},{13,1},{2,6},{6,10},{... | collective-permute-start | bytes 393224 | tf_op jit(solution)/shard_map/ppermute | solution.py:71
  138.6 8.5 %collective-permute-start.23 = (bf16[16,4096]{1,0:T(8,128)(2,1)S(1)}, bf16[16,4096]{1,0:T(8,128)(2,1)S(1)}, u32[]{:S(2)}, u32[]{:S(2)}) collective-permute-start(bf16[16,4096]{1,0:T(8,128)(2,1)S(1)} %get-tuple-element.50), channel_id=1, source_target_pairs={{0,12},{4,0},{8,4},{12,8},{1,13},{5,1},{9,5},{13,9},{2,14},{6,2},{... | collective-permute-start | bytes 393224 | tf_op jit(solution)/shard_map/ppermute | solution.py:71
  141.9 11.9 %collective-permute-start.24 = (bf16[16,4096]{1,0:T(8,128)(2,1)S(1)}, bf16[16,4096]{1,0:T(8,128)(2,1)S(1)}, u32[]{:S(2)}, u32[]{:S(2)}) collective-permute-start(bf16[16,4096]{1,0:T(8,128)(2,1)S(1)} %get-tuple-element.51), channel_id=1, source_target_pairs={{0,8},{4,12},{8,0},{12,4},{1,9},{5,13},{9,1},{13,5},{2,10},{6,14},... | collective-permute-start | bytes 393224 | tf_op jit(solution)/shard_map/ppermute | solution.py:71
  142.5 11.4 %collective-permute-start.26 = (bf16[128,1024]{1,0:T(8,128)(2,1)S(1)}, bf16[128,1024]{1,0:T(8,128)(2,1)S(1)}, u32[]{:S(2)}, u32[]{:S(2)}) collective-permute-start(bf16[128,1024]{1,0:T(8,128)(2,1)S(1)} %activate.3.refs_1_.refs_3_), channel_id=1, source_target_pairs={{0,2},{2,0},{1,3},{3,1},{4,6},{6,4},{5,7},{7,5},{8,10},{10,8},{9,1... | collective-permute-start | bytes 786440 | tf_op jit(solution)/shard_map/ppermute | solution.py:71
  160.0 8.2 %collective-permute-start.28 = (bf16[16,4096]{1,0:T(8,128)(2,1)S(1)}, bf16[16,4096]{1,0:T(8,128)(2,1)S(1)}, u32[]{:S(2)}, u32[]{:S(2)}) collective-permute-start(bf16[16,4096]{1,0:T(8,128)(2,1)S(1)} %get-tuple-element.55), channel_id=1, source_target_pairs={{0,4},{4,8},{8,12},{12,0},{1,5},{5,9},{9,13},{13,1},{2,6},{6,10},{... | collective-permute-start | bytes 393224 | tf_op jit(solution)/shard_map/ppermute | solution.py:71
  160.0 10.2 %collective-permute-start.29 = (bf16[16,4096]{1,0:T(8,128)(2,1)S(1)}, bf16[16,4096]{1,0:T(8,128)(2,1)S(1)}, u32[]{:S(2)}, u32[]{:S(2)}) collective-permute-start(bf16[16,4096]{1,0:T(8,128)(2,1)S(1)} %get-tuple-element.56), channel_id=1, source_target_pairs={{0,12},{4,0},{8,4},{12,8},{1,13},{5,1},{9,5},{13,9},{2,14},{6,2},{... | collective-permute-start | bytes 393224 | tf_op jit(solution)/shard_map/ppermute | solution.py:71
  163.9 9.8 %collective-permute-start.30 = (bf16[16,4096]{1,0:T(8,128)(2,1)S(1)}, bf16[16,4096]{1,0:T(8,128)(2,1)S(1)}, u32[]{:S(2)}, u32[]{:S(2)}) collective-permute-start(bf16[16,4096]{1,0:T(8,128)(2,1)S(1)} %get-tuple-element.57), channel_id=1, source_target_pairs={{0,8},{4,12},{8,0},{12,4},{1,9},{5,13},{9,1},{13,5},{2,10},{6,14},... | collective-permute-start | bytes 393224 | tf_op jit(solution)/shard_map/ppermute | solution.py:71
  (10 other events, 68.5 us)
where the time goes:
time: 175 us; the launch traced here: 174 us
  Pallas kernels  73.7 us (42%)
  waiting for transfers between devices  58 us (33%)
  starting transfers between devices  38 us (22%)
  other arithmetic  3.37 us (2%)
    pallas_call x31, Pallas kernels, run(): pl.pallas_call(body, name=name, in_specs=list(in_specs) + [IN_PLACE] * m,...  73.7 us
    ppermute x31, waiting for transfers between devices, shift(): return lax.ppermute(x, axis, [(i, (i + k) % size) for i in range(size)])  58 us
    ppermute x31, starting transfers between devices, shift(): return lax.ppermute(x, axis, [(i, (i + k) % size) for i in range(size)])  38 us
  transfers between devices with their start and end apart: 31, of which 15 were waited for; matrix products, arithmetic and copies ran while one was open for 1% of the time, Pallas kernels for 33%

commit v1 on v0

--- a/solution.py
+++ b/solution.py
@@ -17,7 +17,7 @@
 F32 = jnp.float32
 VMEM_LIMIT = 48 * 1024 * 1024
 STAT_ROWS = 32
-PIECES = 1
+PIECES = 4
 LOG2E = 1.4426950408889634
 LN2 = 0.6931471805599453
 
@@ -73,6 +73,8 @@
 
 def attention_kernel(
     heads,
+    group,
+    ahead,
     groups,
     where_ref,
     sample_hbm,
@@ -93,8 +95,11 @@
     rows, span = suffix_ref.shape[1:3]
     lanes_s = rows * heads
     scale2 = HD**-0.5 * LOG2E
-    q_at = pl.ds(pl.multiple_of(where_ref[0] * (heads * HD), HD), heads * HD)
-    kv_at = pl.ds(pl.multiple_of(where_ref[1] * HD, HD), HD)
+    n_ctx = q_hbm.shape[1] // (heads * HD)
+    chunk = lax.rem(where_ref[0] + ahead, n_ctx)
+    kv = lax.div(chunk * heads, group)
+    q_at = pl.ds(pl.multiple_of(chunk * (heads * HD), HD), heads * HD)
+    kv_at = pl.ds(pl.multiple_of(kv * HD, HD), HD)
     numbers = [
         pltpu.make_async_copy(sample_hbm, sample_ref, number_sems.at[0]),
         pltpu.make_async_copy(length_hbm, length_ref, number_sems.at[1]),
@@ -126,7 +131,7 @@
     ids = jnp.zeros((lanes_s, 1), jnp.int32)
     lens = jnp.zeros((1, lanes_s), jnp.int32)
     for r in range(rows):
-        sample = lax.rem(sample_ref[where_ref[2] + r], samples)
+        sample = lax.rem(sample_ref[where_ref[3] + r], samples)
         ids = jnp.where(column == r, sample, ids)
         lens = jnp.where(across == r, length_ref[sample], lens)
     shape = (lanes_s, heads * samples)
@@ -209,13 +214,15 @@
     msg_ref[heads * HD :, :] = stats.astype(BF16)
 
 
-def attention_piece(where, cache_sample, suffix_length, queries, prefix, suffix, heads):
+def attention_piece(
+    ahead, where, cache_sample, suffix_length, queries, prefix, suffix, heads, group
+):
     samples = queries.shape[0]
     block, rows, span = prefix.shape[1], suffix.shape[1], suffix.shape[2]
     groups = 4 if rows % 4 == 0 else 1
     return run(
         "attention",
-        functools.partial(attention_kernel, heads, groups),
+        functools.partial(attention_kernel, heads, group, ahead, groups),
         [SCALARS] + [IN_PLACE] * 5,
         [where, cache_sample, suffix_length, queries, prefix, suffix],
         out_specs=WHOLE,
@@ -431,26 +438,35 @@
             jax.ShapeDtypeStruct((rows, width), BF16),
             jax.ShapeDtypeStruct((rows, width + HD), BF16),
         ],
-    )
-
-
-def finish_kernel(*refs):
-    total = refs[0][...].astype(F32)
-    for ref in refs[1:-1]:
+        cost_estimate=cost(8),
+    )
+
+
+def finish_kernel(above, *refs):
+    terms, out_ref = refs[above:-1], refs[-1]
+    total = terms[0][...].astype(F32)
+    for ref in terms[1:]:
         total = total + ref[...].astype(F32)
-    refs[-1][...] = total.astype(refs[-1].dtype)
-
-
-def finish(pieces):
+    row = 0
+    for ref in refs[:above]:
+        out_ref[row : row + ref.shape[0], :] = ref[...]
+        row += ref.shape[0]
+    out_ref[row:, :] = total.astype(out_ref.dtype)
+
+
+def finish(pieces, above=()):
     total = pieces[-1]
     for i in reversed(range(len(pieces) - 1)):
+        on_top = list(above) if i == 0 else []
+        rows, width = total.shape
+        shape = (sum(x.shape[0] for x in on_top) + rows, width)
         total = run(
             "finish",
-            finish_kernel,
-            [WHOLE] * 2,
-            [total, pieces[i]],
+            functools.partial(finish_kernel, len(on_top)),
+            [WHOLE] * (len(on_top) + 2),
+            [*on_top, total, pieces[i]],
             out_specs=WHOLE,
-            out_shape=jax.ShapeDtypeStruct(total.shape, F32 if i else BF16),
+            out_shape=jax.ShapeDtypeStruct(shape, F32 if i else BF16),
         )
     return total
 
@@ -519,7 +535,7 @@
         scratch_shapes=[pltpu.VMEM((rows, depth), BF16), pltpu.VMEM((rows, 2 * units), F32)]
         + [pltpu.VMEM((chunks, tile, units), BF16)] * 2
         + [pltpu.SemaphoreType.DMA((chunks,))] * 2,
-        cost_estimate=cost(2 + 4.2 * units / 1024),
+        cost_estimate=cost(6 if dtype == BF16 else 1),
     )
 
 
@@ -640,19 +656,16 @@
     heads = kv_heads * group // n_ctx
 
     base = (ctx * n_smp + smp) * rows
+    where = jnp.stack([ctx, smp, head, base])
     pieces = []
     for k in far_first(n_ctx) + [0]:
-        chunk = (ctx + k) % n_ctx
-        kv = chunk * heads // group
-        at = jnp.stack([chunk, kv, base])
         piece = attention_piece(
-            at, cache_sample, suffix_length, queries, prefix, suffix, heads
+            k, where, cache_sample, suffix_length, queries, prefix, suffix, heads, group
         )
         pieces.append(shift(piece, "ctx", n_ctx, k) if k else piece)
 
     parts = 2 if own_rows % 32 == 0 else 1
     step = own_rows // parts
-    where = jnp.stack([ctx, smp, head])
     every = range(parts)
     others = range(1, n_smp)
     attn = merge(pieces, heads)
@@ -664,7 +677,7 @@
     ]
     units = gate_matrix.shape[1] // n_smp
     states, rows, full = [None] * parts, [None] * parts, [None] * parts
-    received, own, hidden, theirs = ([None] * parts for _ in range(4))
+    received, own, hidden, theirs, acc = ([None] * parts for _ in range(5))
     sums = [None] * parts
     done = []
 
@@ -716,19 +729,18 @@
             state_step(p + 1)
             own_step(p)
             hidden_step(p)
+            acc[p] = down_step(p, 0, 1, None)
             continue
         own_step(p)
-        for q in range(p):
-            keep, *sends = down_step(q, 0, n_smp, None)
-            sums[q] = add_heads(keep, send_heads(sends, 1), 0, n_ctx)
+        by_head = [down_step(q, 1, n_smp - 1, acc[q]) for q in range(p)]
         hidden_step(p)
-        acc = down_step(p, 0, 1, None)
+        for q, (keep, *sends) in enumerate(by_head):
+            sums[q] = add_heads(keep, send_heads(sends, 1), 0, n_ctx, done)
+        acc[p] = down_step(p, 0, 1, None)
         outs = [finish([states[q], *send_sums(sums[q])]) for q in range(p)]
-        done = done + outs
-        keep, *sends = down_step(p, 1, n_smp - 1, acc)
-    sums[-1] = add_heads(keep, send_heads(sends, PIECES), 0, n_ctx)
-    outs.append(finish([states[-1], *send_sums(sums[-1])]))
-    return jnp.concatenate(outs, axis=0)
+        keep, *sends = down_step(p, 1, n_smp - 1, acc[p])
+    sums[-1] = add_heads(keep, send_heads(sends, PIECES), 0, n_ctx, outs)
+    return finish([states[-1], *send_sums(sums[-1])], outs)
 
 
 def solution(mesh):

time: 175 us -> 167 us (0.954)
  waiting for transfers between devices: 58 us -> 46 us
  starting transfers between devices: 38 us -> 44 us
  other arithmetic: 3.37 us -> 0.55 us
    ppermute x31 -> x34, waiting for transfers between devices: 58 us -> 46 us  [shift(): return lax.ppermute(x, axis, [(i, (i + k) % size) for i in range(size)])]
    ppermute x31 -> x34, starting transfers between devices: 38 us -> 44 us  [shift(): return lax.ppermute(x, axis, [(i, (i + k) % size) for i in range(size)])]
    another operation x6 -> x1, other arithmetic: 2.65 us -> 0.55 us  [on_device(): where = jnp.stack([ctx, smp, head, base])]
    pallas_call x31 -> x32, Pallas kernels: 73.7 us -> 75.1 us  [run(): pl.pallas_call(body, name=name, in_specs=list(in_specs) + [IN_PLACE] * m,...]
  transfers between devices with their start and end apart: 31 -> 34, of which waited for: 15 -> 16; matrix products, arithmetic and copies ran while one was open for 1% -> 0% of each run, Pallas kernels for 33% -> 37%
where the time goes in v1:
time: 167 us
  Pallas kernels  75.1 us (45%)
  waiting for transfers between devices  46 us (28%)
  starting transfers between devices  44 us (26%)
    pallas_call x32, Pallas kernels, run(): pl.pallas_call(body, name=name, in_specs=list(in_specs) + [IN_PLACE] * m,...  75.1 us
    ppermute x34, waiting for transfers between devices, shift(): return lax.ppermute(x, axis, [(i, (i + k) % size) for i in range(size)])  46 us
    ppermute x34, starting transfers between devices, shift(): return lax.ppermute(x, axis, [(i, (i + k) % size) for i in range(size)])  44 us
  transfers between devices with their start and end apart: 34, of which 16 were waited for; matrix products, arithmetic and copies ran while one was open for 0% of the time, Pallas kernels for 37%

profile of v1, /device:TPU:0, one launch (start us, length us, event | category | flops | bytes accessed | tf_op | source)
XLA Modules:
  0.0 167.1 jit_solution(16684617606992444103)
XLA Ops:
  0.6 6.5 %attention.4 = bf16[1056,128]{1,0:T(8,128)(2,1)} custom-call(s32[4]{0:T(128)} %pad_add_fusion.refs_0_, s32[256]{0:T(256)} %refs_1_.7, s32[128]{0:T(128)} %refs_2_.9, bf16[128,4096]{1,0:T(8,128)(2,1)} %bitcast.20, bf16[2,1024,512]{2,1,0:T(8,128)(2,1)} %bitcast.16, bf16[2,32,128,512]{3,2,1,0:T(8,128)(2,1)} %bitcast.12), custom_call_target="tpu_custom_call" | custom-call | flops 5500000256 | bytes 18000000 | tf_op jit(solution)/shard_map/attention/pallas_call | solution.py:46
  7.0 4.1 %collective-permute-start = (bf16[1056,128]{1,0:T(8,128)(2,1)}, bf16[1056,128]{1,0:T(8,128)(2,1)S(1)}, u32[]{:S(2)}, u32[]{:S(2)}) collective-permute-start(bf16[1056,128]{1,0:T(8,128)(2,1)} %attention.4), channel_id=1, source_target_pairs={{0,8},{4,12},{8,0},{12,4},{1,9},{5,13},{9,1},{13,5},{2,10},{6,14},... | collective-permute-start | bytes 811016 | tf_op jit(solution)/shard_map/ppermute | solution.py:71
  11.1 6.5 %attention.5 = bf16[1056,128]{1,0:T(8,128)(2,1)} custom-call(s32[4]{0:T(128)} %pad_add_fusion.refs_0_, s32[256]{0:T(256)} %refs_1_.7, s32[128]{0:T(128)} %refs_2_.9, bf16[128,4096]{1,0:T(8,128)(2,1)} %bitcast.21, bf16[2,1024,512]{2,1,0:T(8,128)(2,1)} %bitcast.17, bf16[2,32,128,512]{3,2,1,0:T(8,128)(2,1)} %bitcast.13), custom_call_target="tpu_custom_call" | custom-call | flops 5500000256 | bytes 18000000 | tf_op jit(solution)/shard_map/attention/pallas_call | solution.py:46
  19.3 6.5 %attention.6 = bf16[1056,128]{1,0:T(8,128)(2,1)} custom-call(s32[4]{0:T(128)} %pad_add_fusion.refs_0_, s32[256]{0:T(256)} %refs_1_.7, s32[128]{0:T(128)} %refs_2_.9, bf16[128,4096]{1,0:T(8,128)(2,1)} %bitcast.22, bf16[2,1024,512]{2,1,0:T(8,128)(2,1)} %bitcast.18, bf16[2,32,128,512]{3,2,1,0:T(8,128)(2,1)} %bitcast.14), custom_call_target="tpu_custom_call" | custom-call | flops 5500000256 | bytes 18000000 | tf_op jit(solution)/shard_map/attention/pallas_call | solution.py:46
  28.2 6.5 %attention.7.refs_3_ = bf16[1056,128]{1,0:T(8,128)(2,1)} custom-call(s32[4]{0:T(128)} %pad_add_fusion.refs_0_, s32[256]{0:T(256)} %refs_1_.7, s32[128]{0:T(128)} %refs_2_.9, bf16[128,4096]{1,0:T(8,128)(2,1)} %bitcast.23, bf16[2,1024,512]{2,1,0:T(8,128)(2,1)} %bitcast.19, bf16[2,32,128,512]{3,2,1,0:T(8,128)(2,1)} %bitcast.15), custom_call_target="tpu_custom_call" | custom-call | flops 5500000256 | bytes 18000000 | tf_op jit(solution)/shard_map/attention/pallas_call | solution.py:46
  38.1 6.1 %collective-permute-done.3.refs_2_ = bf16[128,1024]{1,0:T(8,128)(2,1)S(1)} collective-permute-done((bf16[128,1024]{1,0:T(8,128)(2,1)S(1)}, bf16[128,1024]{1,0:T(8,128)(2,1)S(1)}, u32[]{:S(2)}, u32[]{:S(2)}) %collective-permute-start.3) | collective-permute-done | bytes 262176 | tf_op jit(solution)/shard_map/ppermute | solution.py:71
  44.2 5.0 %project.1 = (bf16[64,4096]{1,0:T(8,128)(2,1)S(1)}, bf16[64,4096]{1,0:T(8,128)(2,1)S(1)}, bf16[128,4096]{1,0:T(8,128)(2,1)S(1)}) custom-call(s32[4]{0:T(128)S(1)} %copy-done, bf16[128,1024]{1,0:T(8,128)(2,1)S(1)} %merge.1.refs_1_, bf16[128,1024]{1,0:T(8,128)(2,1)S(1)} %collective-permute-done.3.refs_2_, bf16[1,1024,4096]{2,1,0:T(8,128)(2,1)} %refs_3_.7), custom_call_target="tpu_custom_call" | custom-call | flops 5500000256 | bytes 18000000 | tf_op jit(solution)/shard_map/project/pallas_call | solution.py:46
  52.1 3.3 %collective-permute-start.5 = (bf16[16,4096]{1,0:T(8,128)(2,1)S(1)}, bf16[16,4096]{1,0:T(8,128)(2,1)S(1)}, u32[]{:S(2)}, u32[]{:S(2)}) collective-permute-start(bf16[16,4096]{1,0:T(8,128)(2,1)S(1)} %get-tuple-element.35), channel_id=1, source_target_pairs={{0,8},{4,12},{8,0},{12,4},{1,9},{5,13},{9,1},{13,5},{2,10},{6,14},... | collective-permute-start | bytes 393224 | tf_op jit(solution)/shard_map/ppermute | solution.py:71
  57.5 5.4 %collective-permute-done.5.refs_1_ = bf16[16,4096]{1,0:T(8,128)(2,1)S(1)} collective-permute-done((bf16[16,4096]{1,0:T(8,128)(2,1)S(1)}, bf16[16,4096]{1,0:T(8,128)(2,1)S(1)}, u32[]{:S(2)}, u32[]{:S(2)}) %collective-permute-start.5) | collective-permute-done | bytes 131104 | tf_op jit(solution)/shard_map/ppermute | solution.py:71
  65.9 2.8 %collective-permute-start.10 = (bf16[16,4224]{1,0:T(8,128)(2,1)S(1)}, bf16[16,4224]{1,0:T(8,128)(2,1)S(1)}, u32[]{:S(2)}, u32[]{:S(2)}) collective-permute-start(bf16[16,4224]{1,0:T(8,128)(2,1)S(1)} %get-tuple-element.38.refs_0_), channel_id=1, source_target_pairs={{0,12},{4,0},{8,4},{12,8},{1,13},{5,1},{9,5},{13,9},{2,14},{6,2},{... | collective-permute-start | bytes 405512 | tf_op jit(solution)/shard_map/ppermute | solution.py:71
  72.3 10.2 %collective-permute-done.9.refs_2_ = bf16[16,4224]{1,0:T(8,128)(2,1)S(1)} collective-permute-done((bf16[16,4224]{1,0:T(8,128)(2,1)S(1)}, bf16[16,4224]{1,0:T(8,128)(2,1)S(1)}, u32[]{:S(2)}, u32[]{:S(2)}) %collective-permute-start.9) | collective-permute-done | bytes 135200 | tf_op jit(solution)/shard_map/ppermute | solution.py:71
  85.6 6.3 %gate_up.4.refs_6_ = bf16[128,2176]{1,0:T(8,128)(2,1)S(1)} custom-call(s32[1]{0:T(128)} %bitcast.refs_0_, bf16[64,4224]{1,0:T(8,128)(2,1)S(1)} %join.2.refs_1_, bf16[64,4224]{1,0:T(8,128)(2,1)S(1)} %collective-permute-done.11.refs_2_, bf16[4096,2048]{1,0:T(8,128)(2,1)} %refs_3_.11, bf16[4096,2048]{1,0:T(8,128)(2,1)} %refs_4_.7, ...), custom_call_target="tpu_custom_call" | custom-call | flops 6600000000 | bytes 21600000 | tf_op jit(solution)/shard_map/gate_up/pallas_call | solution.py:46
  98.6 6.4 %gate_up.5.refs_0_.refs_2_ = f32[128,2176]{1,0:T(8,128)S(1)} custom-call(s32[1]{0:T(128)} %bitcast.1.refs_0_, bf16[64,4224]{1,0:T(8,128)(2,1)S(1)} %join.2.refs_1_, bf16[64,4224]{1,0:T(8,128)(2,1)S(1)} %collective-permute-done.11.refs_2_, bf16[4096,2048]{1,0:T(8,128)(2,1)} %refs_3_.11, bf16[4096,2048]{1,0:T(8,128)(2,1)} %refs_4_.7, ...), custom_call_target="tpu_custom_call" | custom-call | flops 1100000000 | bytes 3600000 | tf_op jit(solution)/shard_map/gate_up/pallas_call | solution.py:46
  106.6 4.0 %down.4.refs_4_.refs_5_.refs_2_ = f32[128,4096]{1,0:T(8,128)S(1)} custom-call(s32[1]{0:T(128)} %bitcast.9.refs_0_, bf16[128,1024]{1,0:T(8,128)(2,1)S(1)} %activate.2.refs_1_.refs_3_, bf16[2048,4096]{1,0:T(8,128)(2,1)} %refs_3_.13, bf16[128,1024]{1,0:T(8,128)(2,1)S(1)} %activate.2.refs_1_.refs_3_), custom_call_target="tpu_custom_call" | custom-call | flops 4400000000 | bytes 14400000 | tf_op jit(solution)/shard_map/down/pallas_call | solution.py:46
  112.9 6.3 %gate_up.6.refs_5_ = bf16[128,2176]{1,0:T(8,128)(2,1)S(1)} custom-call(s32[1]{0:T(128)} %bitcast.refs_0_, bf16[64,4224]{1,0:T(8,128)(2,1)S(1)} %join.3.refs_1_, bf16[64,4224]{1,0:T(8,128)(2,1)S(1)} %collective-permute-done.20.refs_2_, bf16[4096,2048]{1,0:T(8,128)(2,1)} %refs_3_.11, bf16[4096,2048]{1,0:T(8,128)(2,1)} %refs_4_.7, ...), custom_call_target="tpu_custom_call" | custom-call | flops 6600000000 | bytes 21600000 | tf_op jit(solution)/shard_map/gate_up/pallas_call | solution.py:46
  120.8 6.4 %gate_up.7.refs_4_.refs_0_ = f32[128,2176]{1,0:T(8,128)S(1)} custom-call(s32[1]{0:T(128)} %bitcast.1.refs_0_, bf16[64,4224]{1,0:T(8,128)(2,1)S(1)} %join.3.refs_1_, bf16[64,4224]{1,0:T(8,128)(2,1)S(1)} %collective-permute-done.20.refs_2_, bf16[4096,2048]{1,0:T(8,128)(2,1)} %refs_3_.11, bf16[4096,2048]{1,0:T(8,128)(2,1)} %refs_4_.7, ...), custom_call_target="tpu_custom_call" | custom-call | flops 1100000000 | bytes 3600000 | tf_op jit(solution)/shard_map/gate_up/pallas_call | solution.py:46
  127.2 4.0 %down.5 = (bf16[64,4096]{1,0:T(8,128)(2,1)S(1)}, bf16[64,4096]{1,0:T(8,128)(2,1)S(1)}) custom-call(s32[1]{0:T(128)} %bitcast.refs_0_, bf16[128,1024]{1,0:T(8,128)(2,1)S(1)} %collective-permute-done.16.refs_1_, f32[128,4096]{1,0:T(8,128)S(1)} %down.4.refs_4_.refs_5_.refs_2_, bf16[2048,4096]{1,0:T(8,128)(2,1)} %refs_3_.13, f32[128,2176]{1,0:T(8,128)S(1)} %gate_up.7.refs_4_.refs_0_), custom_call_target="tpu_custom_call" | custom-call | flops 4400000000 | bytes 14400000 | tf_op jit(solution)/shard_map/down/pallas_call | solution.py:46
  131.3 2.7 %collective-permute-done.22.refs_1_ = bf16[128,2176]{1,0:T(8,128)(2,1)S(1)} collective-permute-done((bf16[128,2176]{1,0:T(8,128)(2,1)S(1)}, bf16[128,2176]{1,0:T(8,128)(2,1)S(1)}, u32[]{:S(2)}, u32[]{:S(2)}) %collective-permute-start.22) | collective-permute-done | bytes 557088 | tf_op jit(solution)/shard_map/ppermute | solution.py:71
  136.8 3.1 %collective-permute-start.24 = (bf16[16,4096]{1,0:T(8,128)(2,1)S(1)}, bf16[16,4096]{1,0:T(8,128)(2,1)S(1)}, u32[]{:S(2)}, u32[]{:S(2)}) collective-permute-start(bf16[16,4096]{1,0:T(8,128)(2,1)S(1)} %get-tuple-element.50), channel_id=1, source_target_pairs={{0,12},{4,0},{8,4},{12,8},{1,13},{5,1},{9,5},{13,9},{2,14},{6,2},{... | collective-permute-start | bytes 393224 | tf_op jit(solution)/shard_map/ppermute | solution.py:71
  140.0 4.0 %down.6.refs_2_.refs_4_ = f32[128,4096]{1,0:T(8,128)S(1)} custom-call(s32[1]{0:T(128)} %bitcast.9.refs_0_, bf16[128,1024]{1,0:T(8,128)(2,1)S(1)} %activate.3.refs_2_.refs_1_.refs_3_, bf16[2048,4096]{1,0:T(8,128)(2,1)} %refs_3_.13, bf16[128,1024]{1,0:T(8,128)(2,1)S(1)} %activate.3.refs_2_.refs_1_.refs_3_), custom_call_target="tpu_custom_call" | custom-call | flops 4400000000 | bytes 14400000 | tf_op jit(solution)/shard_map/down/pallas_call | solution.py:46
  144.0 4.0 %down.7 = (bf16[64,4096]{1,0:T(8,128)(2,1)S(1)}, bf16[64,4096]{1,0:T(8,128)(2,1)S(1)}) custom-call(s32[1]{0:T(128)} %bitcast.refs_0_, bf16[128,1024]{1,0:T(8,128)(2,1)S(1)} %collective-permute-done.26.refs_1_, f32[128,4096]{1,0:T(8,128)S(1)} %down.6.refs_2_.refs_4_, bf16[2048,4096]{1,0:T(8,128)(2,1)} %refs_3_.13, f32[128,4096]{1,0:T(8,128)S(1)} %down.6.refs_2_.refs_4_), custom_call_target="tpu_custom_call" | custom-call | flops 4400000000 | bytes 14400000 | tf_op jit(solution)/shard_map/down/pallas_call | solution.py:46
  151.3 3.4 %collective-permute-start.32 = (bf16[16,4096]{1,0:T(8,128)(2,1)S(1)}, bf16[16,4096]{1,0:T(8,128)(2,1)S(1)}, u32[]{:S(2)}, u32[]{:S(2)}) collective-permute-start(bf16[16,4096]{1,0:T(8,128)(2,1)S(1)} %get-tuple-element.56), channel_id=1, source_target_pairs={{0,12},{4,0},{8,4},{12,8},{1,13},{5,1},{9,5},{13,9},{2,14},{6,2},{... | collective-permute-start | bytes 393224 | tf_op jit(solution)/shard_map/ppermute | solution.py:71
  155.2 3.9 %collective-permute-done.31.refs_0_ = bf16[16,4096]{1,0:T(8,128)(2,1)S(1)} collective-permute-done((bf16[16,4096]{1,0:T(8,128)(2,1)S(1)}, bf16[16,4096]{1,0:T(8,128)(2,1)S(1)}, u32[]{:S(2)}, u32[]{:S(2)}) %collective-permute-start.31) | collective-permute-done | bytes 131104 | tf_op jit(solution)/shard_map/ppermute | solution.py:71
  160.2 6.0 %collective-permute-done.33.refs_1_ = bf16[16,4096]{1,0:T(8,128)(2,1)S(1)} collective-permute-done((bf16[16,4096]{1,0:T(8,128)(2,1)S(1)}, bf16[16,4096]{1,0:T(8,128)(2,1)S(1)}, u32[]{:S(2)}, u32[]{:S(2)}) %collective-permute-start.33) | collective-permute-done | bytes 131104 | tf_op jit(solution)/shard_map/ppermute | solution.py:71
  (87 shorter events, 43.4 us)
Async XLA Ops:
  7.0 27.7 %collective-permute-start = (bf16[1056,128]{1,0:T(8,128)(2,1)}, bf16[1056,128]{1,0:T(8,128)(2,1)S(1)}, u32[]{:S(2)}, u32[]{:S(2)}) collective-permute-start(bf16[1056,128]{1,0:T(8,128)(2,1)} %attention.4), channel_id=1, source_target_pairs={{0,8},{4,12},{8,0},{12,4},{1,9},{5,13},{9,1},{13,5},{2,10},{6,14},... | collective-permute-start | bytes 811016 | tf_op jit(solution)/shard_map/ppermute | solution.py:71
  17.6 17.1 %collective-permute-start.1 = (bf16[1056,128]{1,0:T(8,128)(2,1)}, bf16[1056,128]{1,0:T(8,128)(2,1)S(1)}, u32[]{:S(2)}, u32[]{:S(2)}) collective-permute-start(bf16[1056,128]{1,0:T(8,128)(2,1)} %attention.5), channel_id=1, source_target_pairs={{0,4},{4,8},{8,12},{12,0},{1,5},{5,9},{9,13},{13,1},{2,6},{6,10},{... | collective-permute-start | bytes 811016 | tf_op jit(solution)/shard_map/ppermute | solution.py:71
  25.7 9.5 %collective-permute-start.2 = (bf16[1056,128]{1,0:T(8,128)(2,1)}, bf16[1056,128]{1,0:T(8,128)(2,1)S(1)}, u32[]{:S(2)}, u32[]{:S(2)}) collective-permute-start(bf16[1056,128]{1,0:T(8,128)(2,1)} %attention.6), channel_id=1, source_target_pairs={{0,12},{4,0},{8,4},{12,8},{1,13},{5,1},{9,5},{13,9},{2,14},{6,2},{... | collective-permute-start | bytes 811016 | tf_op jit(solution)/shard_map/ppermute | solution.py:71
  36.5 7.7 %collective-permute-start.3 = (bf16[128,1024]{1,0:T(8,128)(2,1)S(1)}, bf16[128,1024]{1,0:T(8,128)(2,1)S(1)}, u32[]{:S(2)}, u32[]{:S(2)}) collective-permute-start(bf16[128,1024]{1,0:T(8,128)(2,1)S(1)} %merge.1.refs_1_), channel_id=1, source_target_pairs={{0,2},{2,0},{1,3},{3,1},{4,6},{6,4},{5,7},{7,5},{8,10},{10,8},{9,1... | collective-permute-start | bytes 786440 | tf_op jit(solution)/shard_map/ppermute | solution.py:71
  52.1 10.7 %collective-permute-start.5 = (bf16[16,4096]{1,0:T(8,128)(2,1)S(1)}, bf16[16,4096]{1,0:T(8,128)(2,1)S(1)}, u32[]{:S(2)}, u32[]{:S(2)}) collective-permute-start(bf16[16,4096]{1,0:T(8,128)(2,1)S(1)} %get-tuple-element.35), channel_id=1, source_target_pairs={{0,8},{4,12},{8,0},{12,4},{1,9},{5,13},{9,1},{13,5},{2,10},{6,14},... | collective-permute-start | bytes 393224 | tf_op jit(solution)/shard_map/ppermute | solution.py:71
  56.2 9.5 %collective-permute-start.7 = (bf16[16,4096]{1,0:T(8,128)(2,1)S(1)}, bf16[16,4096]{1,0:T(8,128)(2,1)S(1)}, u32[]{:S(2)}, u32[]{:S(2)}) collective-permute-start(bf16[16,4096]{1,0:T(8,128)(2,1)S(1)} %get-tuple-element.37), channel_id=1, source_target_pairs={{0,4},{4,8},{8,12},{12,0},{1,5},{5,9},{9,13},{13,1},{2,6},{6,10},{... | collective-permute-start | bytes 393224 | tf_op jit(solution)/shard_map/ppermute | solution.py:71
  68.7 13.8 %collective-permute-start.9 = (bf16[16,4224]{1,0:T(8,128)(2,1)S(1)}, bf16[16,4224]{1,0:T(8,128)(2,1)S(1)}, u32[]{:S(2)}, u32[]{:S(2)}) collective-permute-start(bf16[16,4224]{1,0:T(8,128)(2,1)S(1)} %get-tuple-element.38.refs_0_), channel_id=1, source_target_pairs={{0,8},{4,12},{8,0},{12,4},{1,9},{5,13},{9,1},{13,5},{2,10},{6,14},... | collective-permute-start | bytes 405512 | tf_op jit(solution)/shard_map/ppermute | solution.py:71
  70.3 12.2 %collective-permute-start.8 = (bf16[16,4224]{1,0:T(8,128)(2,1)S(1)}, bf16[16,4224]{1,0:T(8,128)(2,1)S(1)}, u32[]{:S(2)}, u32[]{:S(2)}) collective-permute-start(bf16[16,4224]{1,0:T(8,128)(2,1)S(1)} %get-tuple-element.38.refs_0_), channel_id=1, source_target_pairs={{0,4},{4,8},{8,12},{12,0},{1,5},{5,9},{9,13},{13,1},{2,6},{6,10},{... | collective-permute-start | bytes 405512 | tf_op jit(solution)/shard_map/ppermute | solution.py:71
  82.8 10.8 %collective-permute-start.12 = (bf16[16,4096]{1,0:T(8,128)(2,1)S(1)}, bf16[16,4096]{1,0:T(8,128)(2,1)S(1)}, u32[]{:S(2)}, u32[]{:S(2)}) collective-permute-start(bf16[16,4096]{1,0:T(8,128)(2,1)S(1)} %get-tuple-element.42), channel_id=1, source_target_pairs={{0,8},{4,12},{8,0},{12,4},{1,9},{5,13},{9,1},{13,5},{2,10},{6,14},... | collective-permute-start | bytes 393224 | tf_op jit(solution)/shard_map/ppermute | solution.py:71
  83.6 11.2 %collective-permute-start.13 = (bf16[16,4096]{1,0:T(8,128)(2,1)S(1)}, bf16[16,4096]{1,0:T(8,128)(2,1)S(1)}, u32[]{:S(2)}, u32[]{:S(2)}) collective-permute-start(bf16[16,4096]{1,0:T(8,128)(2,1)S(1)} %get-tuple-element.43), channel_id=1, source_target_pairs={{0,12},{4,0},{8,4},{12,8},{1,13},{5,1},{9,5},{13,9},{2,14},{6,2},{... | collective-permute-start | bytes 393224 | tf_op jit(solution)/shard_map/ppermute | solution.py:71
  84.1 10.8 %collective-permute-start.14 = (bf16[16,4096]{1,0:T(8,128)(2,1)S(1)}, bf16[16,4096]{1,0:T(8,128)(2,1)S(1)}, u32[]{:S(2)}, u32[]{:S(2)}) collective-permute-start(bf16[16,4096]{1,0:T(8,128)(2,1)S(1)} %get-tuple-element.44), channel_id=1, source_target_pairs={{0,4},{4,8},{8,12},{12,0},{1,5},{5,9},{9,13},{13,1},{2,6},{6,10},{... | collective-permute-start | bytes 393224 | tf_op jit(solution)/shard_map/ppermute | solution.py:71
  92.0 14.2 %collective-permute-start.15 = (bf16[128,2176]{1,0:T(8,128)(2,1)S(1)}, bf16[128,2176]{1,0:T(8,128)(2,1)S(1)}, u32[]{:S(2)}, u32[]{:S(2)}) collective-permute-start(bf16[128,2176]{1,0:T(8,128)(2,1)S(1)} %gate_up.4.refs_6_), channel_id=1, source_target_pairs={{0,2},{2,0},{1,3},{3,1},{4,6},{6,4},{5,7},{7,5},{8,10},{10,8},{9,1... | collective-permute-start | bytes 1671176 | tf_op jit(solution)/shard_map/ppermute | solution.py:71
  95.0 15.5 %collective-permute-start.19 = (bf16[16,4224]{1,0:T(8,128)(2,1)S(1)}, bf16[16,4224]{1,0:T(8,128)(2,1)S(1)}, u32[]{:S(2)}, u32[]{:S(2)}) collective-permute-start(bf16[16,4224]{1,0:T(8,128)(2,1)S(1)} %get-tuple-element.46.refs_0_), channel_id=1, source_target_pairs={{0,12},{4,0},{8,4},{12,8},{1,13},{5,1},{9,5},{13,9},{2,14},{6,2},{... | collective-permute-start | bytes 405512 | tf_op jit(solution)/shard_map/ppermute | solution.py:71
  96.0 14.8 %collective-permute-start.18 = (bf16[16,4224]{1,0:T(8,128)(2,1)S(1)}, bf16[16,4224]{1,0:T(8,128)(2,1)S(1)}, u32[]{:S(2)}, u32[]{:S(2)}) collective-permute-start(bf16[16,4224]{1,0:T(8,128)(2,1)S(1)} %get-tuple-element.46.refs_0_), channel_id=1, source_target_pairs={{0,8},{4,12},{8,0},{12,4},{1,9},{5,13},{9,1},{13,5},{2,10},{6,14},... | collective-permute-start | bytes 405512 | tf_op jit(solution)/shard_map/ppermute | solution.py:71
  98.6 12.2 %collective-permute-start.17 = (bf16[16,4224]{1,0:T(8,128)(2,1)S(1)}, bf16[16,4224]{1,0:T(8,128)(2,1)S(1)}, u32[]{:S(2)}, u32[]{:S(2)}) collective-permute-start(bf16[16,4224]{1,0:T(8,128)(2,1)S(1)} %get-tuple-element.46.refs_0_), channel_id=1, source_target_pairs={{0,4},{4,8},{8,12},{12,0},{1,5},{5,9},{9,13},{13,1},{2,6},{6,10},{... | collective-permute-start | bytes 405512 | tf_op jit(solution)/shard_map/ppermute | solution.py:71
  111.0 16.2 %collective-permute-start.16 = (bf16[128,1024]{1,0:T(8,128)(2,1)S(1)}, bf16[128,1024]{1,0:T(8,128)(2,1)S(1)}, u32[]{:S(2)}, u32[]{:S(2)}) collective-permute-start(bf16[128,1024]{1,0:T(8,128)(2,1)S(1)} %activate.2.refs_1_.refs_3_), channel_id=1, source_target_pairs={{0,2},{2,0},{1,3},{3,1},{4,6},{6,4},{5,7},{7,5},{8,10},{10,8},{9,1... | collective-permute-start | bytes 786440 | tf_op jit(solution)/shard_map/ppermute | solution.py:71
  119.2 14.7 %collective-permute-start.22 = (bf16[128,2176]{1,0:T(8,128)(2,1)S(1)}, bf16[128,2176]{1,0:T(8,128)(2,1)S(1)}, u32[]{:S(2)}, u32[]{:S(2)}) collective-permute-start(bf16[128,2176]{1,0:T(8,128)(2,1)S(1)} %gate_up.6.refs_5_), channel_id=1, source_target_pairs={{0,2},{2,0},{1,3},{3,1},{4,6},{6,4},{5,7},{7,5},{8,10},{10,8},{9,1... | collective-permute-start | bytes 1671176 | tf_op jit(solution)/shard_map/ppermute | solution.py:71
  134.3 9.7 %collective-permute-start.26 = (bf16[128,1024]{1,0:T(8,128)(2,1)S(1)}, bf16[128,1024]{1,0:T(8,128)(2,1)S(1)}, u32[]{:S(2)}, u32[]{:S(2)}) collective-permute-start(bf16[128,1024]{1,0:T(8,128)(2,1)S(1)} %activate.3.refs_2_.refs_1_.refs_3_), channel_id=1, source_target_pairs={{0,2},{2,0},{1,3},{3,1},{4,6},{6,4},{5,7},{7,5},{8,10},{10,8},{9,1... | collective-permute-start | bytes 786440 | tf_op jit(solution)/shard_map/ppermute | solution.py:71
  136.0 12.6 %collective-permute-start.23 = (bf16[16,4096]{1,0:T(8,128)(2,1)S(1)}, bf16[16,4096]{1,0:T(8,128)(2,1)S(1)}, u32[]{:S(2)}, u32[]{:S(2)}) collective-permute-start(bf16[16,4096]{1,0:T(8,128)(2,1)S(1)} %get-tuple-element.49), channel_id=1, source_target_pairs={{0,4},{4,8},{8,12},{12,0},{1,5},{5,9},{9,13},{13,1},{2,6},{6,10},{... | collective-permute-start | bytes 393224 | tf_op jit(solution)/shard_map/ppermute | solution.py:71
  136.8 11.9 %collective-permute-start.24 = (bf16[16,4096]{1,0:T(8,128)(2,1)S(1)}, bf16[16,4096]{1,0:T(8,128)(2,1)S(1)}, u32[]{:S(2)}, u32[]{:S(2)}) collective-permute-start(bf16[16,4096]{1,0:T(8,128)(2,1)S(1)} %get-tuple-element.50), channel_id=1, source_target_pairs={{0,12},{4,0},{8,4},{12,8},{1,13},{5,1},{9,5},{13,9},{2,14},{6,2},{... | collective-permute-start | bytes 393224 | tf_op jit(solution)/shard_map/ppermute | solution.py:71
  139.9 10.7 %collective-permute-start.25 = (bf16[16,4096]{1,0:T(8,128)(2,1)S(1)}, bf16[16,4096]{1,0:T(8,128)(2,1)S(1)}, u32[]{:S(2)}, u32[]{:S(2)}) collective-permute-start(bf16[16,4096]{1,0:T(8,128)(2,1)S(1)} %get-tuple-element.51), channel_id=1, source_target_pairs={{0,8},{4,12},{8,0},{12,4},{1,9},{5,13},{9,1},{13,5},{2,10},{6,14},... | collective-permute-start | bytes 393224 | tf_op jit(solution)/shard_map/ppermute | solution.py:71
  150.8 8.3 %collective-permute-start.31 = (bf16[16,4096]{1,0:T(8,128)(2,1)S(1)}, bf16[16,4096]{1,0:T(8,128)(2,1)S(1)}, u32[]{:S(2)}, u32[]{:S(2)}) collective-permute-start(bf16[16,4096]{1,0:T(8,128)(2,1)S(1)} %get-tuple-element.55), channel_id=1, source_target_pairs={{0,4},{4,8},{8,12},{12,0},{1,5},{5,9},{9,13},{13,1},{2,6},{6,10},{... | collective-permute-start | bytes 393224 | tf_op jit(solution)/shard_map/ppermute | solution.py:71
  151.3 8.9 %collective-permute-start.32 = (bf16[16,4096]{1,0:T(8,128)(2,1)S(1)}, bf16[16,4096]{1,0:T(8,128)(2,1)S(1)}, u32[]{:S(2)}, u32[]{:S(2)}) collective-permute-start(bf16[16,4096]{1,0:T(8,128)(2,1)S(1)} %get-tuple-element.56), channel_id=1, source_target_pairs={{0,12},{4,0},{8,4},{12,8},{1,13},{5,1},{9,5},{13,9},{2,14},{6,2},{... | collective-permute-start | bytes 393224 | tf_op jit(solution)/shard_map/ppermute | solution.py:71
  154.7 11.6 %collective-permute-start.33 = (bf16[16,4096]{1,0:T(8,128)(2,1)S(1)}, bf16[16,4096]{1,0:T(8,128)(2,1)S(1)}, u32[]{:S(2)}, u32[]{:S(2)}) collective-permute-start(bf16[16,4096]{1,0:T(8,128)(2,1)S(1)} %get-tuple-element.57), channel_id=1, source_target_pairs={{0,8},{4,12},{8,0},{12,4},{1,9},{5,13},{9,1},{13,5},{2,10},{6,14},... | collective-permute-start | bytes 393224 | tf_op jit(solution)/shard_map/ppermute | solution.py:71
  (14 other events, 105.5 us)

commit v2 on v1

--- a/solution.py
+++ b/solution.py
@@ -603,7 +603,7 @@
 def down(blocks, xs, w_down, acc, last, n_head, after):
     rows, units = xs[0].shape
     width = w_down.shape[1]
-    chunks = 4
+    chunks = 8
     tile = width // chunks
     n = len(xs)
     args = list(xs) + ([] if acc is None else [acc])
@@ -671,10 +671,11 @@
     attn = merge(pieces, heads)
     gathered = [attn] + [shift(attn, "smp", n_smp, k) for k in others]
     by_head = project(where, gathered, w_out, n_ctx, n_head, own_rows, parts)
-    recv = send_heads(by_head[parts:], 1)
-    all_sums = [
-        add_heads(by_head[p], recv, p * by_head[p].shape[0], n_ctx) for p in every
-    ]
+    all_sums = []
+    for p in every:
+        per = by_head[p].shape[0]
+        sends = [x[p * per : (p + 1) * per] for x in by_head[parts:]]
+        all_sums.append(add_heads(by_head[p], send_heads(sends, 1), 0, n_ctx))
     units = gate_matrix.shape[1] // n_smp
     states, rows, full = [None] * parts, [None] * parts, [None] * parts
     received, own, hidden, theirs, acc = ([None] * parts for _ in range(5))

time: 167 us -> 166 us (level)
    ppermute x34 -> x35, waiting for transfers between devices: 46 us -> 45.5 us  [shift(): return lax.ppermute(x, axis, [(i, (i + k) % size) for i in range(size)])]
    ppermute x34 -> x35, starting transfers between devices: 44 us -> 43.7 us  [shift(): return lax.ppermute(x, axis, [(i, (i + k) % size) for i in range(size)])]
  transfers between devices with their start and end apart: 34 -> 35, of which waited for: 16 -> 17; matrix products, arithmetic and copies ran while one was open for 0% -> 0% of each run, Pallas kernels for 37% -> 37%
where the time goes in v2:
time: 166 us
  Pallas kernels  74.7 us (45%)
  waiting for transfers between devices  45.5 us (27%)
  starting transfers between devices  43.7 us (26%)
    pallas_call x32, Pallas kernels, run(): pl.pallas_call(body, name=name, in_specs=list(in_specs) + [IN_PLACE] * m,...  74.7 us
    ppermute x35, waiting for transfers between devices, shift(): return lax.ppermute(x, axis, [(i, (i + k) % size) for i in range(size)])  45.5 us
    ppermute x35, starting transfers between devices, shift(): return lax.ppermute(x, axis, [(i, (i + k) % size) for i in range(size)])  43.7 us
  transfers between devices with their start and end apart: 35, of which 17 were waited for; matrix products, arithmetic and copies ran while one was open for 0% of the time, Pallas kernels for 37%

profile of v2, /device:TPU:0, one launch (start us, length us, event | category | flops | bytes accessed | tf_op | source)
XLA Modules:
  0.0 166.2 jit_solution(11523561152819342592)
XLA Ops:
  0.7 6.5 %attention.4 = bf16[1056,128]{1,0:T(8,128)(2,1)} custom-call(s32[4]{0:T(128)} %pad_add_fusion.refs_0_, s32[256]{0:T(256)} %refs_1_.7, s32[128]{0:T(128)} %refs_2_.9, bf16[128,4096]{1,0:T(8,128)(2,1)} %bitcast.20, bf16[2,1024,512]{2,1,0:T(8,128)(2,1)} %bitcast.16, bf16[2,32,128,512]{3,2,1,0:T(8,128)(2,1)} %bitcast.12), custom_call_target="tpu_custom_call" | custom-call | flops 5500000256 | bytes 18000000 | tf_op jit(solution)/shard_map/attention/pallas_call | solution.py:46
  7.1 4.1 %collective-permute-start = (bf16[1056,128]{1,0:T(8,128)(2,1)}, bf16[1056,128]{1,0:T(8,128)(2,1)S(1)}, u32[]{:S(2)}, u32[]{:S(2)}) collective-permute-start(bf16[1056,128]{1,0:T(8,128)(2,1)} %attention.4), channel_id=1, source_target_pairs={{0,8},{4,12},{8,0},{12,4},{1,9},{5,13},{9,1},{13,5},{2,10},{6,14},... | collective-permute-start | bytes 811016 | tf_op jit(solution)/shard_map/ppermute | solution.py:71
  11.2 6.5 %attention.5 = bf16[1056,128]{1,0:T(8,128)(2,1)} custom-call(s32[4]{0:T(128)} %pad_add_fusion.refs_0_, s32[256]{0:T(256)} %refs_1_.7, s32[128]{0:T(128)} %refs_2_.9, bf16[128,4096]{1,0:T(8,128)(2,1)} %bitcast.21, bf16[2,1024,512]{2,1,0:T(8,128)(2,1)} %bitcast.17, bf16[2,32,128,512]{3,2,1,0:T(8,128)(2,1)} %bitcast.13), custom_call_target="tpu_custom_call" | custom-call | flops 5500000256 | bytes 18000000 | tf_op jit(solution)/shard_map/attention/pallas_call | solution.py:46
  19.3 6.5 %attention.6 = bf16[1056,128]{1,0:T(8,128)(2,1)} custom-call(s32[4]{0:T(128)} %pad_add_fusion.refs_0_, s32[256]{0:T(256)} %refs_1_.7, s32[128]{0:T(128)} %refs_2_.9, bf16[128,4096]{1,0:T(8,128)(2,1)} %bitcast.22, bf16[2,1024,512]{2,1,0:T(8,128)(2,1)} %bitcast.18, bf16[2,32,128,512]{3,2,1,0:T(8,128)(2,1)} %bitcast.14), custom_call_target="tpu_custom_call" | custom-call | flops 5500000256 | bytes 18000000 | tf_op jit(solution)/shard_map/attention/pallas_call | solution.py:46
  28.3 6.5 %attention.7.refs_3_ = bf16[1056,128]{1,0:T(8,128)(2,1)} custom-call(s32[4]{0:T(128)} %pad_add_fusion.refs_0_, s32[256]{0:T(256)} %refs_1_.7, s32[128]{0:T(128)} %refs_2_.9, bf16[128,4096]{1,0:T(8,128)(2,1)} %bitcast.23, bf16[2,1024,512]{2,1,0:T(8,128)(2,1)} %bitcast.19, bf16[2,32,128,512]{3,2,1,0:T(8,128)(2,1)} %bitcast.15), custom_call_target="tpu_custom_call" | custom-call | flops 5500000256 | bytes 18000000 | tf_op jit(solution)/shard_map/attention/pallas_call | solution.py:46
  38.2 6.1 %collective-permute-done.3.refs_2_ = bf16[128,1024]{1,0:T(8,128)(2,1)S(1)} collective-permute-done((bf16[128,1024]{1,0:T(8,128)(2,1)S(1)}, bf16[128,1024]{1,0:T(8,128)(2,1)S(1)}, u32[]{:S(2)}, u32[]{:S(2)}) %collective-permute-start.3) | collective-permute-done | bytes 262176 | tf_op jit(solution)/shard_map/ppermute | solution.py:71
  44.3 5.0 %project.1 = (bf16[64,4096]{1,0:T(8,128)(2,1)S(1)}, bf16[64,4096]{1,0:T(8,128)(2,1)S(1)}, bf16[128,4096]{1,0:T(8,128)(2,1)S(1)}) custom-call(s32[4]{0:T(128)S(1)} %copy-done, bf16[128,1024]{1,0:T(8,128)(2,1)S(1)} %merge.1.refs_1_, bf16[128,1024]{1,0:T(8,128)(2,1)S(1)} %collective-permute-done.3.refs_2_, bf16[1,1024,4096]{2,1,0:T(8,128)(2,1)} %refs_3_.7), custom_call_target="tpu_custom_call" | custom-call | flops 5500000256 | bytes 18000000 | tf_op jit(solution)/shard_map/project/pallas_call | solution.py:46
  51.5 3.3 %collective-permute-start.5 = (bf16[16,4096]{1,0:T(8,128)(2,1)S(1)}, bf16[16,4096]{1,0:T(8,128)(2,1)S(1)}, u32[]{:S(2)}, u32[]{:S(2)}) collective-permute-start(bf16[16,4096]{1,0:T(8,128)(2,1)S(1)} %get-tuple-element.35), channel_id=1, source_target_pairs={{0,8},{4,12},{8,0},{12,4},{1,9},{5,13},{9,1},{13,5},{2,10},{6,14},... | collective-permute-start | bytes 393224 | tf_op jit(solution)/shard_map/ppermute | solution.py:71
  56.9 5.4 %collective-permute-done.5.refs_1_ = bf16[16,4096]{1,0:T(8,128)(2,1)S(1)} collective-permute-done((bf16[16,4096]{1,0:T(8,128)(2,1)S(1)}, bf16[16,4096]{1,0:T(8,128)(2,1)S(1)}, u32[]{:S(2)}, u32[]{:S(2)}) %collective-permute-start.5) | collective-permute-done | bytes 131104 | tf_op jit(solution)/shard_map/ppermute | solution.py:71
  65.3 2.8 %collective-permute-start.10 = (bf16[16,4224]{1,0:T(8,128)(2,1)S(1)}, bf16[16,4224]{1,0:T(8,128)(2,1)S(1)}, u32[]{:S(2)}, u32[]{:S(2)}) collective-permute-start(bf16[16,4224]{1,0:T(8,128)(2,1)S(1)} %get-tuple-element.38.refs_0_), channel_id=1, source_target_pairs={{0,12},{4,0},{8,4},{12,8},{1,13},{5,1},{9,5},{13,9},{2,14},{6,2},{... | collective-permute-start | bytes 405512 | tf_op jit(solution)/shard_map/ppermute | solution.py:71
  71.8 10.1 %collective-permute-done.9.refs_2_ = bf16[16,4224]{1,0:T(8,128)(2,1)S(1)} collective-permute-done((bf16[16,4224]{1,0:T(8,128)(2,1)S(1)}, bf16[16,4224]{1,0:T(8,128)(2,1)S(1)}, u32[]{:S(2)}, u32[]{:S(2)}) %collective-permute-start.9) | collective-permute-done | bytes 135200 | tf_op jit(solution)/shard_map/ppermute | solution.py:71
  85.1 6.4 %gate_up.4.refs_6_ = bf16[128,2176]{1,0:T(8,128)(2,1)S(1)} custom-call(s32[1]{0:T(128)} %bitcast.refs_0_, bf16[64,4224]{1,0:T(8,128)(2,1)S(1)} %join.2.refs_1_, bf16[64,4224]{1,0:T(8,128)(2,1)S(1)} %collective-permute-done.11.refs_2_, bf16[4096,2048]{1,0:T(8,128)(2,1)} %refs_3_.11, bf16[4096,2048]{1,0:T(8,128)(2,1)} %refs_4_.7, ...), custom_call_target="tpu_custom_call" | custom-call | flops 6600000000 | bytes 21600000 | tf_op jit(solution)/shard_map/gate_up/pallas_call | solution.py:46
  98.1 6.4 %gate_up.5.refs_0_.refs_2_ = f32[128,2176]{1,0:T(8,128)S(1)} custom-call(s32[1]{0:T(128)} %bitcast.1.refs_0_, bf16[64,4224]{1,0:T(8,128)(2,1)S(1)} %join.2.refs_1_, bf16[64,4224]{1,0:T(8,128)(2,1)S(1)} %collective-permute-done.11.refs_2_, bf16[4096,2048]{1,0:T(8,128)(2,1)} %refs_3_.11, bf16[4096,2048]{1,0:T(8,128)(2,1)} %refs_4_.7, ...), custom_call_target="tpu_custom_call" | custom-call | flops 1100000000 | bytes 3600000 | tf_op jit(solution)/shard_map/gate_up/pallas_call | solution.py:46
  106.0 3.9 %down.4.refs_4_.refs_5_.refs_2_ = f32[128,4096]{1,0:T(8,128)S(1)} custom-call(s32[1]{0:T(128)} %bitcast.9.refs_0_, bf16[128,1024]{1,0:T(8,128)(2,1)S(1)} %activate.2.refs_1_.refs_3_, bf16[2048,4096]{1,0:T(8,128)(2,1)} %refs_3_.13, bf16[128,1024]{1,0:T(8,128)(2,1)S(1)} %activate.2.refs_1_.refs_3_), custom_call_target="tpu_custom_call" | custom-call | flops 4400000000 | bytes 14400000 | tf_op jit(solution)/shard_map/down/pallas_call | solution.py:46
  112.3 6.4 %gate_up.6.refs_5_ = bf16[128,2176]{1,0:T(8,128)(2,1)S(1)} custom-call(s32[1]{0:T(128)} %bitcast.refs_0_, bf16[64,4224]{1,0:T(8,128)(2,1)S(1)} %join.3.refs_1_, bf16[64,4224]{1,0:T(8,128)(2,1)S(1)} %collective-permute-done.21.refs_2_, bf16[4096,2048]{1,0:T(8,128)(2,1)} %refs_3_.11, bf16[4096,2048]{1,0:T(8,128)(2,1)} %refs_4_.7, ...), custom_call_target="tpu_custom_call" | custom-call | flops 6600000000 | bytes 21600000 | tf_op jit(solution)/shard_map/gate_up/pallas_call | solution.py:46
  120.2 6.4 %gate_up.7.refs_4_.refs_0_ = f32[128,2176]{1,0:T(8,128)S(1)} custom-call(s32[1]{0:T(128)} %bitcast.1.refs_0_, bf16[64,4224]{1,0:T(8,128)(2,1)S(1)} %join.3.refs_1_, bf16[64,4224]{1,0:T(8,128)(2,1)S(1)} %collective-permute-done.21.refs_2_, bf16[4096,2048]{1,0:T(8,128)(2,1)} %refs_3_.11, bf16[4096,2048]{1,0:T(8,128)(2,1)} %refs_4_.7, ...), custom_call_target="tpu_custom_call" | custom-call | flops 1100000000 | bytes 3600000 | tf_op jit(solution)/shard_map/gate_up/pallas_call | solution.py:46
  126.6 3.9 %down.5 = (bf16[64,4096]{1,0:T(8,128)(2,1)S(1)}, bf16[64,4096]{1,0:T(8,128)(2,1)S(1)}) custom-call(s32[1]{0:T(128)} %bitcast.refs_0_, bf16[128,1024]{1,0:T(8,128)(2,1)S(1)} %collective-permute-done.17.refs_1_, f32[128,4096]{1,0:T(8,128)S(1)} %down.4.refs_4_.refs_5_.refs_2_, bf16[2048,4096]{1,0:T(8,128)(2,1)} %refs_3_.13, f32[128,2176]{1,0:T(8,128)S(1)} %gate_up.7.refs_4_.refs_0_), custom_call_target="tpu_custom_call" | custom-call | flops 4400000000 | bytes 14400000 | tf_op jit(solution)/shard_map/down/pallas_call | solution.py:46
  130.6 2.8 %collective-permute-done.23.refs_1_ = bf16[128,2176]{1,0:T(8,128)(2,1)S(1)} collective-permute-done((bf16[128,2176]{1,0:T(8,128)(2,1)S(1)}, bf16[128,2176]{1,0:T(8,128)(2,1)S(1)}, u32[]{:S(2)}, u32[]{:S(2)}) %collective-permute-start.23) | collective-permute-done | bytes 557088 | tf_op jit(solution)/shard_map/ppermute | solution.py:71
  136.1 3.2 %collective-permute-start.25 = (bf16[16,4096]{1,0:T(8,128)(2,1)S(1)}, bf16[16,4096]{1,0:T(8,128)(2,1)S(1)}, u32[]{:S(2)}, u32[]{:S(2)}) collective-permute-start(bf16[16,4096]{1,0:T(8,128)(2,1)S(1)} %get-tuple-element.50), channel_id=1, source_target_pairs={{0,12},{4,0},{8,4},{12,8},{1,13},{5,1},{9,5},{13,9},{2,14},{6,2},{... | collective-permute-start | bytes 393224 | tf_op jit(solution)/shard_map/ppermute | solution.py:71
  139.3 3.9 %down.6.refs_2_.refs_4_ = f32[128,4096]{1,0:T(8,128)S(1)} custom-call(s32[1]{0:T(128)} %bitcast.9.refs_0_, bf16[128,1024]{1,0:T(8,128)(2,1)S(1)} %activate.3.refs_2_.refs_1_.refs_3_, bf16[2048,4096]{1,0:T(8,128)(2,1)} %refs_3_.13, bf16[128,1024]{1,0:T(8,128)(2,1)S(1)} %activate.3.refs_2_.refs_1_.refs_3_), custom_call_target="tpu_custom_call" | custom-call | flops 4400000000 | bytes 14400000 | tf_op jit(solution)/shard_map/down/pallas_call | solution.py:46
  143.2 3.9 %down.7 = (bf16[64,4096]{1,0:T(8,128)(2,1)S(1)}, bf16[64,4096]{1,0:T(8,128)(2,1)S(1)}) custom-call(s32[1]{0:T(128)} %bitcast.refs_0_, bf16[128,1024]{1,0:T(8,128)(2,1)S(1)} %collective-permute-done.27.refs_1_, f32[128,4096]{1,0:T(8,128)S(1)} %down.6.refs_2_.refs_4_, bf16[2048,4096]{1,0:T(8,128)(2,1)} %refs_3_.13, f32[128,4096]{1,0:T(8,128)S(1)} %down.6.refs_2_.refs_4_), custom_call_target="tpu_custom_call" | custom-call | flops 4400000000 | bytes 14400000 | tf_op jit(solution)/shard_map/down/pallas_call | solution.py:46
  150.4 3.6 %collective-permute-start.33 = (bf16[16,4096]{1,0:T(8,128)(2,1)S(1)}, bf16[16,4096]{1,0:T(8,128)(2,1)S(1)}, u32[]{:S(2)}, u32[]{:S(2)}) collective-permute-start(bf16[16,4096]{1,0:T(8,128)(2,1)S(1)} %get-tuple-element.56), channel_id=1, source_target_pairs={{0,12},{4,0},{8,4},{12,8},{1,13},{5,1},{9,5},{13,9},{2,14},{6,2},{... | collective-permute-start | bytes 393224 | tf_op jit(solution)/shard_map/ppermute | solution.py:71
  154.4 4.0 %collective-permute-done.32.refs_0_ = bf16[16,4096]{1,0:T(8,128)(2,1)S(1)} collective-permute-done((bf16[16,4096]{1,0:T(8,128)(2,1)S(1)}, bf16[16,4096]{1,0:T(8,128)(2,1)S(1)}, u32[]{:S(2)}, u32[]{:S(2)}) %collective-permute-start.32) | collective-permute-done | bytes 131104 | tf_op jit(solution)/shard_map/ppermute | solution.py:71
  159.5 5.9 %collective-permute-done.34.refs_1_ = bf16[16,4096]{1,0:T(8,128)(2,1)S(1)} collective-permute-done((bf16[16,4096]{1,0:T(8,128)(2,1)S(1)}, bf16[16,4096]{1,0:T(8,128)(2,1)S(1)}, u32[]{:S(2)}, u32[]{:S(2)}) %collective-permute-start.34) | collective-permute-done | bytes 131104 | tf_op jit(solution)/shard_map/ppermute | solution.py:71
  (90 shorter events, 42.5 us)
Async XLA Ops:
  7.1 27.7 %collective-permute-start = (bf16[1056,128]{1,0:T(8,128)(2,1)}, bf16[1056,128]{1,0:T(8,128)(2,1)S(1)}, u32[]{:S(2)}, u32[]{:S(2)}) collective-permute-start(bf16[1056,128]{1,0:T(8,128)(2,1)} %attention.4), channel_id=1, source_target_pairs={{0,8},{4,12},{8,0},{12,4},{1,9},{5,13},{9,1},{13,5},{2,10},{6,14},... | collective-permute-start | bytes 811016 | tf_op jit(solution)/shard_map/ppermute | solution.py:71
  17.7 17.1 %collective-permute-start.1 = (bf16[1056,128]{1,0:T(8,128)(2,1)}, bf16[1056,128]{1,0:T(8,128)(2,1)S(1)}, u32[]{:S(2)}, u32[]{:S(2)}) collective-permute-start(bf16[1056,128]{1,0:T(8,128)(2,1)} %attention.5), channel_id=1, source_target_pairs={{0,4},{4,8},{8,12},{12,0},{1,5},{5,9},{9,13},{13,1},{2,6},{6,10},{... | collective-permute-start | bytes 811016 | tf_op jit(solution)/shard_map/ppermute | solution.py:71
  25.8 9.5 %collective-permute-start.2 = (bf16[1056,128]{1,0:T(8,128)(2,1)}, bf16[1056,128]{1,0:T(8,128)(2,1)S(1)}, u32[]{:S(2)}, u32[]{:S(2)}) collective-permute-start(bf16[1056,128]{1,0:T(8,128)(2,1)} %attention.6), channel_id=1, source_target_pairs={{0,12},{4,0},{8,4},{12,8},{1,13},{5,1},{9,5},{13,9},{2,14},{6,2},{... | collective-permute-start | bytes 811016 | tf_op jit(solution)/shard_map/ppermute | solution.py:71
  51.5 10.7 %collective-permute-start.5 = (bf16[16,4096]{1,0:T(8,128)(2,1)S(1)}, bf16[16,4096]{1,0:T(8,128)(2,1)S(1)}, u32[]{:S(2)}, u32[]{:S(2)}) collective-permute-start(bf16[16,4096]{1,0:T(8,128)(2,1)S(1)} %get-tuple-element.35), channel_id=1, source_target_pairs={{0,8},{4,12},{8,0},{12,4},{1,9},{5,13},{9,1},{13,5},{2,10},{6,14},... | collective-permute-start | bytes 393224 | tf_op jit(solution)/shard_map/ppermute | solution.py:71
  55.6 9.5 %collective-permute-start.7 = (bf16[16,4096]{1,0:T(8,128)(2,1)S(1)}, bf16[16,4096]{1,0:T(8,128)(2,1)S(1)}, u32[]{:S(2)}, u32[]{:S(2)}) collective-permute-start(bf16[16,4096]{1,0:T(8,128)(2,1)S(1)} %get-tuple-element.37), channel_id=1, source_target_pairs={{0,4},{4,8},{8,12},{12,0},{1,5},{5,9},{9,13},{13,1},{2,6},{6,10},{... | collective-permute-start | bytes 393224 | tf_op jit(solution)/shard_map/ppermute | solution.py:71
  68.1 13.8 %collective-permute-start.9 = (bf16[16,4224]{1,0:T(8,128)(2,1)S(1)}, bf16[16,4224]{1,0:T(8,128)(2,1)S(1)}, u32[]{:S(2)}, u32[]{:S(2)}) collective-permute-start(bf16[16,4224]{1,0:T(8,128)(2,1)S(1)} %get-tuple-element.38.refs_0_), channel_id=1, source_target_pairs={{0,8},{4,12},{8,0},{12,4},{1,9},{5,13},{9,1},{13,5},{2,10},{6,14},... | collective-permute-start | bytes 405512 | tf_op jit(solution)/shard_map/ppermute | solution.py:71
  69.8 12.1 %collective-permute-start.8 = (bf16[16,4224]{1,0:T(8,128)(2,1)S(1)}, bf16[16,4224]{1,0:T(8,128)(2,1)S(1)}, u32[]{:S(2)}, u32[]{:S(2)}) collective-permute-start(bf16[16,4224]{1,0:T(8,128)(2,1)S(1)} %get-tuple-element.38.refs_0_), channel_id=1, source_target_pairs={{0,4},{4,8},{8,12},{12,0},{1,5},{5,9},{9,13},{13,1},{2,6},{6,10},{... | collective-permute-start | bytes 405512 | tf_op jit(solution)/shard_map/ppermute | solution.py:71
  71.7 10.3 %collective-permute-start.12 = (bf16[64,4096]{1,0:T(8,128)(2,1)S(1)}, bf16[64,4096]{1,0:T(8,128)(2,1)S(1)}, u32[]{:S(2)}, u32[]{:S(2)}) collective-permute-start(bf16[64,4096]{1,0:T(8,128)(2,1)S(1)} %get-tuple-element.59), channel_id=1, source_target_pairs={{0,1},{1,0},{2,3},{3,2},{4,5},{5,4},{6,7},{7,6},{8,9},{9,8},{10,11... | collective-permute-start | bytes 1572872 | tf_op jit(solution)/shard_map/ppermute | solution.py:71
  82.2 10.8 %collective-permute-start.13 = (bf16[16,4096]{1,0:T(8,128)(2,1)S(1)}, bf16[16,4096]{1,0:T(8,128)(2,1)S(1)}, u32[]{:S(2)}, u32[]{:S(2)}) collective-permute-start(bf16[16,4096]{1,0:T(8,128)(2,1)S(1)} %get-tuple-element.42), channel_id=1, source_target_pairs={{0,8},{4,12},{8,0},{12,4},{1,9},{5,13},{9,1},{13,5},{2,10},{6,14},... | collective-permute-start | bytes 393224 | tf_op jit(solution)/shard_map/ppermute | solution.py:71
  83.1 11.2 %collective-permute-start.14 = (bf16[16,4096]{1,0:T(8,128)(2,1)S(1)}, bf16[16,4096]{1,0:T(8,128)(2,1)S(1)}, u32[]{:S(2)}, u32[]{:S(2)}) collective-permute-start(bf16[16,4096]{1,0:T(8,128)(2,1)S(1)} %get-tuple-element.43), channel_id=1, source_target_pairs={{0,12},{4,0},{8,4},{12,8},{1,13},{5,1},{9,5},{13,9},{2,14},{6,2},{... | collective-permute-start | bytes 393224 | tf_op jit(solution)/shard_map/ppermute | solution.py:71
  83.5 10.8 %collective-permute-start.15 = (bf16[16,4096]{1,0:T(8,128)(2,1)S(1)}, bf16[16,4096]{1,0:T(8,128)(2,1)S(1)}, u32[]{:S(2)}, u32[]{:S(2)}) collective-permute-start(bf16[16,4096]{1,0:T(8,128)(2,1)S(1)} %get-tuple-element.44), channel_id=1, source_target_pairs={{0,4},{4,8},{8,12},{12,0},{1,5},{5,9},{9,13},{13,1},{2,6},{6,10},{... | collective-permute-start | bytes 393224 | tf_op jit(solution)/shard_map/ppermute | solution.py:71
  91.5 14.2 %collective-permute-start.16 = (bf16[128,2176]{1,0:T(8,128)(2,1)S(1)}, bf16[128,2176]{1,0:T(8,128)(2,1)S(1)}, u32[]{:S(2)}, u32[]{:S(2)}) collective-permute-start(bf16[128,2176]{1,0:T(8,128)(2,1)S(1)} %gate_up.4.refs_6_), channel_id=1, source_target_pairs={{0,2},{2,0},{1,3},{3,1},{4,6},{6,4},{5,7},{7,5},{8,10},{10,8},{9,1... | collective-permute-start | bytes 1671176 | tf_op jit(solution)/shard_map/ppermute | solution.py:71
  94.5 15.4 %collective-permute-start.20 = (bf16[16,4224]{1,0:T(8,128)(2,1)S(1)}, bf16[16,4224]{1,0:T(8,128)(2,1)S(1)}, u32[]{:S(2)}, u32[]{:S(2)}) collective-permute-start(bf16[16,4224]{1,0:T(8,128)(2,1)S(1)} %get-tuple-element.46.refs_0_), channel_id=1, source_target_pairs={{0,12},{4,0},{8,4},{12,8},{1,13},{5,1},{9,5},{13,9},{2,14},{6,2},{... | collective-permute-start | bytes 405512 | tf_op jit(solution)/shard_map/ppermute | solution.py:71
  95.5 14.8 %collective-permute-start.19 = (bf16[16,4224]{1,0:T(8,128)(2,1)S(1)}, bf16[16,4224]{1,0:T(8,128)(2,1)S(1)}, u32[]{:S(2)}, u32[]{:S(2)}) collective-permute-start(bf16[16,4224]{1,0:T(8,128)(2,1)S(1)} %get-tuple-element.46.refs_0_), channel_id=1, source_target_pairs={{0,8},{4,12},{8,0},{12,4},{1,9},{5,13},{9,1},{13,5},{2,10},{6,14},... | collective-permute-start | bytes 405512 | tf_op jit(solution)/shard_map/ppermute | solution.py:71
  98.1 12.2 %collective-permute-start.18 = (bf16[16,4224]{1,0:T(8,128)(2,1)S(1)}, bf16[16,4224]{1,0:T(8,128)(2,1)S(1)}, u32[]{:S(2)}, u32[]{:S(2)}) collective-permute-start(bf16[16,4224]{1,0:T(8,128)(2,1)S(1)} %get-tuple-element.46.refs_0_), channel_id=1, source_target_pairs={{0,4},{4,8},{8,12},{12,0},{1,5},{5,9},{9,13},{13,1},{2,6},{6,10},{... | collective-permute-start | bytes 405512 | tf_op jit(solution)/shard_map/ppermute | solution.py:71
  110.4 16.2 %collective-permute-start.17 = (bf16[128,1024]{1,0:T(8,128)(2,1)S(1)}, bf16[128,1024]{1,0:T(8,128)(2,1)S(1)}, u32[]{:S(2)}, u32[]{:S(2)}) collective-permute-start(bf16[128,1024]{1,0:T(8,128)(2,1)S(1)} %activate.2.refs_1_.refs_3_), channel_id=1, source_target_pairs={{0,2},{2,0},{1,3},{3,1},{4,6},{6,4},{5,7},{7,5},{8,10},{10,8},{9,1... | collective-permute-start | bytes 786440 | tf_op jit(solution)/shard_map/ppermute | solution.py:71
  118.7 14.7 %collective-permute-start.23 = (bf16[128,2176]{1,0:T(8,128)(2,1)S(1)}, bf16[128,2176]{1,0:T(8,128)(2,1)S(1)}, u32[]{:S(2)}, u32[]{:S(2)}) collective-permute-start(bf16[128,2176]{1,0:T(8,128)(2,1)S(1)} %gate_up.6.refs_5_), channel_id=1, source_target_pairs={{0,2},{2,0},{1,3},{3,1},{4,6},{6,4},{5,7},{7,5},{8,10},{10,8},{9,1... | collective-permute-start | bytes 1671176 | tf_op jit(solution)/shard_map/ppermute | solution.py:71
  133.8 9.4 %collective-permute-start.27 = (bf16[128,1024]{1,0:T(8,128)(2,1)S(1)}, bf16[128,1024]{1,0:T(8,128)(2,1)S(1)}, u32[]{:S(2)}, u32[]{:S(2)}) collective-permute-start(bf16[128,1024]{1,0:T(8,128)(2,1)S(1)} %activate.3.refs_2_.refs_1_.refs_3_), channel_id=1, source_target_pairs={{0,2},{2,0},{1,3},{3,1},{4,6},{6,4},{5,7},{7,5},{8,10},{10,8},{9,1... | collective-permute-start | bytes 786440 | tf_op jit(solution)/shard_map/ppermute | solution.py:71
  135.4 12.3 %collective-permute-start.24 = (bf16[16,4096]{1,0:T(8,128)(2,1)S(1)}, bf16[16,4096]{1,0:T(8,128)(2,1)S(1)}, u32[]{:S(2)}, u32[]{:S(2)}) collective-permute-start(bf16[16,4096]{1,0:T(8,128)(2,1)S(1)} %get-tuple-element.49), channel_id=1, source_target_pairs={{0,4},{4,8},{8,12},{12,0},{1,5},{5,9},{9,13},{13,1},{2,6},{6,10},{... | collective-permute-start | bytes 393224 | tf_op jit(solution)/shard_map/ppermute | solution.py:71
  136.1 11.7 %collective-permute-start.25 = (bf16[16,4096]{1,0:T(8,128)(2,1)S(1)}, bf16[16,4096]{1,0:T(8,128)(2,1)S(1)}, u32[]{:S(2)}, u32[]{:S(2)}) collective-permute-start(bf16[16,4096]{1,0:T(8,128)(2,1)S(1)} %get-tuple-element.50), channel_id=1, source_target_pairs={{0,12},{4,0},{8,4},{12,8},{1,13},{5,1},{9,5},{13,9},{2,14},{6,2},{... | collective-permute-start | bytes 393224 | tf_op jit(solution)/shard_map/ppermute | solution.py:71
  139.3 10.5 %collective-permute-start.26 = (bf16[16,4096]{1,0:T(8,128)(2,1)S(1)}, bf16[16,4096]{1,0:T(8,128)(2,1)S(1)}, u32[]{:S(2)}, u32[]{:S(2)}) collective-permute-start(bf16[16,4096]{1,0:T(8,128)(2,1)S(1)} %get-tuple-element.51), channel_id=1, source_target_pairs={{0,8},{4,12},{8,0},{12,4},{1,9},{5,13},{9,1},{13,5},{2,10},{6,14},... | collective-permute-start | bytes 393224 | tf_op jit(solution)/shard_map/ppermute | solution.py:71
  150.1 8.3 %collective-permute-start.32 = (bf16[16,4096]{1,0:T(8,128)(2,1)S(1)}, bf16[16,4096]{1,0:T(8,128)(2,1)S(1)}, u32[]{:S(2)}, u32[]{:S(2)}) collective-permute-start(bf16[16,4096]{1,0:T(8,128)(2,1)S(1)} %get-tuple-element.55), channel_id=1, source_target_pairs={{0,4},{4,8},{8,12},{12,0},{1,5},{5,9},{9,13},{13,1},{2,6},{6,10},{... | collective-permute-start | bytes 393224 | tf_op jit(solution)/shard_map/ppermute | solution.py:71
  150.4 9.0 %collective-permute-start.33 = (bf16[16,4096]{1,0:T(8,128)(2,1)S(1)}, bf16[16,4096]{1,0:T(8,128)(2,1)S(1)}, u32[]{:S(2)}, u32[]{:S(2)}) collective-permute-start(bf16[16,4096]{1,0:T(8,128)(2,1)S(1)} %get-tuple-element.56), channel_id=1, source_target_pairs={{0,12},{4,0},{8,4},{12,8},{1,13},{5,1},{9,5},{13,9},{2,14},{6,2},{... | collective-permute-start | bytes 393224 | tf_op jit(solution)/shard_map/ppermute | solution.py:71
  154.0 11.4 %collective-permute-start.34 = (bf16[16,4096]{1,0:T(8,128)(2,1)S(1)}, bf16[16,4096]{1,0:T(8,128)(2,1)S(1)}, u32[]{:S(2)}, u32[]{:S(2)}) collective-permute-start(bf16[16,4096]{1,0:T(8,128)(2,1)S(1)} %get-tuple-element.57), channel_id=1, source_target_pairs={{0,8},{4,12},{8,0},{12,4},{1,9},{5,13},{9,1},{13,5},{2,10},{6,14},... | collective-permute-start | bytes 393224 | tf_op jit(solution)/shard_map/ppermute | solution.py:71
  (15 other events, 112.1 us)

commit v3 on v2

--- a/solution.py
+++ b/solution.py
@@ -315,7 +315,7 @@
     n_smp = len(attn)
     samples, depth = attn[0].shape
     width = w_out.shape[2]
-    chunks = 4
+    chunks = 8
     tile = width // chunks
     per = n_ctx * own_rows // parts
     rows = per * parts * n_head

time: 166 us -> 167 us (level)
  no operation moved by 1% of the time
where the time goes in v3:
time: 167 us
  Pallas kernels  75.1 us (45%)
  waiting for transfers between devices  45.5 us (27%)
  starting transfers between devices  43.8 us (26%)
    pallas_call x32, Pallas kernels, run(): pl.pallas_call(body, name=name, in_specs=list(in_specs) + [IN_PLACE] * m,...  75.1 us
    ppermute x35, waiting for transfers between devices, shift(): return lax.ppermute(x, axis, [(i, (i + k) % size) for i in range(size)])  45.5 us
    ppermute x35, starting transfers between devices, shift(): return lax.ppermute(x, axis, [(i, (i + k) % size) for i in range(size)])  43.8 us
  transfers between devices with their start and end apart: 35, of which 17 were waited for; matrix products, arithmetic and copies ran while one was open for 0% of the time, Pallas kernels for 37%

profile of v3, /device:TPU:0, one launch (start us, length us, event | category | flops | bytes accessed | tf_op | source)
XLA Modules:
  0.0 166.5 jit_solution(5753013195681679262)
XLA Ops:
  0.7 6.5 %attention.4 = bf16[1056,128]{1,0:T(8,128)(2,1)} custom-call(s32[4]{0:T(128)} %pad_add_fusion.refs_0_, s32[256]{0:T(256)} %refs_1_.7, s32[128]{0:T(128)} %refs_2_.9, bf16[128,4096]{1,0:T(8,128)(2,1)} %bitcast.20, bf16[2,1024,512]{2,1,0:T(8,128)(2,1)} %bitcast.16, bf16[2,32,128,512]{3,2,1,0:T(8,128)(2,1)} %bitcast.12), custom_call_target="tpu_custom_call" | custom-call | flops 5500000256 | bytes 18000000 | tf_op jit(solution)/shard_map/attention/pallas_call | solution.py:46
  7.1 4.1 %collective-permute-start = (bf16[1056,128]{1,0:T(8,128)(2,1)}, bf16[1056,128]{1,0:T(8,128)(2,1)S(1)}, u32[]{:S(2)}, u32[]{:S(2)}) collective-permute-start(bf16[1056,128]{1,0:T(8,128)(2,1)} %attention.4), channel_id=1, source_target_pairs={{0,8},{4,12},{8,0},{12,4},{1,9},{5,13},{9,1},{13,5},{2,10},{6,14},... | collective-permute-start | bytes 811016 | tf_op jit(solution)/shard_map/ppermute | solution.py:71
  11.2 6.5 %attention.5 = bf16[1056,128]{1,0:T(8,128)(2,1)} custom-call(s32[4]{0:T(128)} %pad_add_fusion.refs_0_, s32[256]{0:T(256)} %refs_1_.7, s32[128]{0:T(128)} %refs_2_.9, bf16[128,4096]{1,0:T(8,128)(2,1)} %bitcast.21, bf16[2,1024,512]{2,1,0:T(8,128)(2,1)} %bitcast.17, bf16[2,32,128,512]{3,2,1,0:T(8,128)(2,1)} %bitcast.13), custom_call_target="tpu_custom_call" | custom-call | flops 5500000256 | bytes 18000000 | tf_op jit(solution)/shard_map/attention/pallas_call | solution.py:46
  19.3 6.5 %attention.6 = bf16[1056,128]{1,0:T(8,128)(2,1)} custom-call(s32[4]{0:T(128)} %pad_add_fusion.refs_0_, s32[256]{0:T(256)} %refs_1_.7, s32[128]{0:T(128)} %refs_2_.9, bf16[128,4096]{1,0:T(8,128)(2,1)} %bitcast.22, bf16[2,1024,512]{2,1,0:T(8,128)(2,1)} %bitcast.18, bf16[2,32,128,512]{3,2,1,0:T(8,128)(2,1)} %bitcast.14), custom_call_target="tpu_custom_call" | custom-call | flops 5500000256 | bytes 18000000 | tf_op jit(solution)/shard_map/attention/pallas_call | solution.py:46
  28.3 6.5 %attention.7.refs_3_ = bf16[1056,128]{1,0:T(8,128)(2,1)} custom-call(s32[4]{0:T(128)} %pad_add_fusion.refs_0_, s32[256]{0:T(256)} %refs_1_.7, s32[128]{0:T(128)} %refs_2_.9, bf16[128,4096]{1,0:T(8,128)(2,1)} %bitcast.23, bf16[2,1024,512]{2,1,0:T(8,128)(2,1)} %bitcast.19, bf16[2,32,128,512]{3,2,1,0:T(8,128)(2,1)} %bitcast.15), custom_call_target="tpu_custom_call" | custom-call | flops 5500000256 | bytes 18000000 | tf_op jit(solution)/shard_map/attention/pallas_call | solution.py:46
  38.2 6.1 %collective-permute-done.3.refs_2_ = bf16[128,1024]{1,0:T(8,128)(2,1)S(1)} collective-permute-done((bf16[128,1024]{1,0:T(8,128)(2,1)S(1)}, bf16[128,1024]{1,0:T(8,128)(2,1)S(1)}, u32[]{:S(2)}, u32[]{:S(2)}) %collective-permute-start.3) | collective-permute-done | bytes 262176 | tf_op jit(solution)/shard_map/ppermute | solution.py:71
  44.3 5.3 %project.1 = (bf16[64,4096]{1,0:T(8,128)(2,1)S(1)}, bf16[64,4096]{1,0:T(8,128)(2,1)S(1)}, bf16[128,4096]{1,0:T(8,128)(2,1)S(1)}) custom-call(s32[4]{0:T(128)S(1)} %copy-done, bf16[128,1024]{1,0:T(8,128)(2,1)S(1)} %merge.1.refs_1_, bf16[128,1024]{1,0:T(8,128)(2,1)S(1)} %collective-permute-done.3.refs_2_, bf16[1,1024,4096]{2,1,0:T(8,128)(2,1)} %refs_3_.7), custom_call_target="tpu_custom_call" | custom-call | flops 5500000256 | bytes 18000000 | tf_op jit(solution)/shard_map/project/pallas_call | solution.py:46
  51.9 3.3 %collective-permute-start.5 = (bf16[16,4096]{1,0:T(8,128)(2,1)S(1)}, bf16[16,4096]{1,0:T(8,128)(2,1)S(1)}, u32[]{:S(2)}, u32[]{:S(2)}) collective-permute-start(bf16[16,4096]{1,0:T(8,128)(2,1)S(1)} %get-tuple-element.35), channel_id=1, source_target_pairs={{0,8},{4,12},{8,0},{12,4},{1,9},{5,13},{9,1},{13,5},{2,10},{6,14},... | collective-permute-start | bytes 393224 | tf_op jit(solution)/shard_map/ppermute | solution.py:71
  57.2 5.4 %collective-permute-done.5.refs_1_ = bf16[16,4096]{1,0:T(8,128)(2,1)S(1)} collective-permute-done((bf16[16,4096]{1,0:T(8,128)(2,1)S(1)}, bf16[16,4096]{1,0:T(8,128)(2,1)S(1)}, u32[]{:S(2)}, u32[]{:S(2)}) %collective-permute-start.5) | collective-permute-done | bytes 131104 | tf_op jit(solution)/shard_map/ppermute | solution.py:71
  65.6 2.8 %collective-permute-start.10 = (bf16[16,4224]{1,0:T(8,128)(2,1)S(1)}, bf16[16,4224]{1,0:T(8,128)(2,1)S(1)}, u32[]{:S(2)}, u32[]{:S(2)}) collective-permute-start(bf16[16,4224]{1,0:T(8,128)(2,1)S(1)} %get-tuple-element.38.refs_0_), channel_id=1, source_target_pairs={{0,12},{4,0},{8,4},{12,8},{1,13},{5,1},{9,5},{13,9},{2,14},{6,2},{... | collective-permute-start | bytes 405512 | tf_op jit(solution)/shard_map/ppermute | solution.py:71
  72.1 10.1 %collective-permute-done.9.refs_2_ = bf16[16,4224]{1,0:T(8,128)(2,1)S(1)} collective-permute-done((bf16[16,4224]{1,0:T(8,128)(2,1)S(1)}, bf16[16,4224]{1,0:T(8,128)(2,1)S(1)}, u32[]{:S(2)}, u32[]{:S(2)}) %collective-permute-start.9) | collective-permute-done | bytes 135200 | tf_op jit(solution)/shard_map/ppermute | solution.py:71
  85.4 6.3 %gate_up.4.refs_6_ = bf16[128,2176]{1,0:T(8,128)(2,1)S(1)} custom-call(s32[1]{0:T(128)} %bitcast.refs_0_, bf16[64,4224]{1,0:T(8,128)(2,1)S(1)} %join.2.refs_1_, bf16[64,4224]{1,0:T(8,128)(2,1)S(1)} %collective-permute-done.11.refs_2_, bf16[4096,2048]{1,0:T(8,128)(2,1)} %refs_3_.11, bf16[4096,2048]{1,0:T(8,128)(2,1)} %refs_4_.7, ...), custom_call_target="tpu_custom_call" | custom-call | flops 6600000000 | bytes 21600000 | tf_op jit(solution)/shard_map/gate_up/pallas_call | solution.py:46
  98.4 6.4 %gate_up.5.refs_0_.refs_2_ = f32[128,2176]{1,0:T(8,128)S(1)} custom-call(s32[1]{0:T(128)} %bitcast.1.refs_0_, bf16[64,4224]{1,0:T(8,128)(2,1)S(1)} %join.2.refs_1_, bf16[64,4224]{1,0:T(8,128)(2,1)S(1)} %collective-permute-done.11.refs_2_, bf16[4096,2048]{1,0:T(8,128)(2,1)} %refs_3_.11, bf16[4096,2048]{1,0:T(8,128)(2,1)} %refs_4_.7, ...), custom_call_target="tpu_custom_call" | custom-call | flops 1100000000 | bytes 3600000 | tf_op jit(solution)/shard_map/gate_up/pallas_call | solution.py:46
  106.3 3.9 %down.4.refs_4_.refs_5_.refs_2_ = f32[128,4096]{1,0:T(8,128)S(1)} custom-call(s32[1]{0:T(128)} %bitcast.9.refs_0_, bf16[128,1024]{1,0:T(8,128)(2,1)S(1)} %activate.2.refs_1_.refs_3_, bf16[2048,4096]{1,0:T(8,128)(2,1)} %refs_3_.13, bf16[128,1024]{1,0:T(8,128)(2,1)S(1)} %activate.2.refs_1_.refs_3_), custom_call_target="tpu_custom_call" | custom-call | flops 4400000000 | bytes 14400000 | tf_op jit(solution)/shard_map/down/pallas_call | solution.py:46
  112.7 6.3 %gate_up.6.refs_5_ = bf16[128,2176]{1,0:T(8,128)(2,1)S(1)} custom-call(s32[1]{0:T(128)} %bitcast.refs_0_, bf16[64,4224]{1,0:T(8,128)(2,1)S(1)} %join.3.refs_1_, bf16[64,4224]{1,0:T(8,128)(2,1)S(1)} %collective-permute-done.21.refs_2_, bf16[4096,2048]{1,0:T(8,128)(2,1)} %refs_3_.11, bf16[4096,2048]{1,0:T(8,128)(2,1)} %refs_4_.7, ...), custom_call_target="tpu_custom_call" | custom-call | flops 6600000000 | bytes 21600000 | tf_op jit(solution)/shard_map/gate_up/pallas_call | solution.py:46
  120.5 6.4 %gate_up.7.refs_4_.refs_0_ = f32[128,2176]{1,0:T(8,128)S(1)} custom-call(s32[1]{0:T(128)} %bitcast.1.refs_0_, bf16[64,4224]{1,0:T(8,128)(2,1)S(1)} %join.3.refs_1_, bf16[64,4224]{1,0:T(8,128)(2,1)S(1)} %collective-permute-done.21.refs_2_, bf16[4096,2048]{1,0:T(8,128)(2,1)} %refs_3_.11, bf16[4096,2048]{1,0:T(8,128)(2,1)} %refs_4_.7, ...), custom_call_target="tpu_custom_call" | custom-call | flops 1100000000 | bytes 3600000 | tf_op jit(solution)/shard_map/gate_up/pallas_call | solution.py:46
  126.9 3.9 %down.5 = (bf16[64,4096]{1,0:T(8,128)(2,1)S(1)}, bf16[64,4096]{1,0:T(8,128)(2,1)S(1)}) custom-call(s32[1]{0:T(128)} %bitcast.refs_0_, bf16[128,1024]{1,0:T(8,128)(2,1)S(1)} %collective-permute-done.17.refs_1_, f32[128,4096]{1,0:T(8,128)S(1)} %down.4.refs_4_.refs_5_.refs_2_, bf16[2048,4096]{1,0:T(8,128)(2,1)} %refs_3_.13, f32[128,2176]{1,0:T(8,128)S(1)} %gate_up.7.refs_4_.refs_0_), custom_call_target="tpu_custom_call" | custom-call | flops 4400000000 | bytes 14400000 | tf_op jit(solution)/shard_map/down/pallas_call | solution.py:46
  130.9 2.8 %collective-permute-done.23.refs_1_ = bf16[128,2176]{1,0:T(8,128)(2,1)S(1)} collective-permute-done((bf16[128,2176]{1,0:T(8,128)(2,1)S(1)}, bf16[128,2176]{1,0:T(8,128)(2,1)S(1)}, u32[]{:S(2)}, u32[]{:S(2)}) %collective-permute-start.23) | collective-permute-done | bytes 557088 | tf_op jit(solution)/shard_map/ppermute | solution.py:71
  136.4 3.2 %collective-permute-start.25 = (bf16[16,4096]{1,0:T(8,128)(2,1)S(1)}, bf16[16,4096]{1,0:T(8,128)(2,1)S(1)}, u32[]{:S(2)}, u32[]{:S(2)}) collective-permute-start(bf16[16,4096]{1,0:T(8,128)(2,1)S(1)} %get-tuple-element.50), channel_id=1, source_target_pairs={{0,12},{4,0},{8,4},{12,8},{1,13},{5,1},{9,5},{13,9},{2,14},{6,2},{... | collective-permute-start | bytes 393224 | tf_op jit(solution)/shard_map/ppermute | solution.py:71
  139.6 3.9 %down.6.refs_2_.refs_4_ = f32[128,4096]{1,0:T(8,128)S(1)} custom-call(s32[1]{0:T(128)} %bitcast.9.refs_0_, bf16[128,1024]{1,0:T(8,128)(2,1)S(1)} %activate.3.refs_2_.refs_1_.refs_3_, bf16[2048,4096]{1,0:T(8,128)(2,1)} %refs_3_.13, bf16[128,1024]{1,0:T(8,128)(2,1)S(1)} %activate.3.refs_2_.refs_1_.refs_3_), custom_call_target="tpu_custom_call" | custom-call | flops 4400000000 | bytes 14400000 | tf_op jit(solution)/shard_map/down/pallas_call | solution.py:46
  143.5 3.9 %down.7 = (bf16[64,4096]{1,0:T(8,128)(2,1)S(1)}, bf16[64,4096]{1,0:T(8,128)(2,1)S(1)}) custom-call(s32[1]{0:T(128)} %bitcast.refs_0_, bf16[128,1024]{1,0:T(8,128)(2,1)S(1)} %collective-permute-done.27.refs_1_, f32[128,4096]{1,0:T(8,128)S(1)} %down.6.refs_2_.refs_4_, bf16[2048,4096]{1,0:T(8,128)(2,1)} %refs_3_.13, f32[128,4096]{1,0:T(8,128)S(1)} %down.6.refs_2_.refs_4_), custom_call_target="tpu_custom_call" | custom-call | flops 4400000000 | bytes 14400000 | tf_op jit(solution)/shard_map/down/pallas_call | solution.py:46
  150.8 3.5 %collective-permute-start.33 = (bf16[16,4096]{1,0:T(8,128)(2,1)S(1)}, bf16[16,4096]{1,0:T(8,128)(2,1)S(1)}, u32[]{:S(2)}, u32[]{:S(2)}) collective-permute-start(bf16[16,4096]{1,0:T(8,128)(2,1)S(1)} %get-tuple-element.56), channel_id=1, source_target_pairs={{0,12},{4,0},{8,4},{12,8},{1,13},{5,1},{9,5},{13,9},{2,14},{6,2},{... | collective-permute-start | bytes 393224 | tf_op jit(solution)/shard_map/ppermute | solution.py:71
  154.7 4.0 %collective-permute-done.32.refs_0_ = bf16[16,4096]{1,0:T(8,128)(2,1)S(1)} collective-permute-done((bf16[16,4096]{1,0:T(8,128)(2,1)S(1)}, bf16[16,4096]{1,0:T(8,128)(2,1)S(1)}, u32[]{:S(2)}, u32[]{:S(2)}) %collective-permute-start.32) | collective-permute-done | bytes 131104 | tf_op jit(solution)/shard_map/ppermute | solution.py:71
  159.8 5.9 %collective-permute-done.34.refs_1_ = bf16[16,4096]{1,0:T(8,128)(2,1)S(1)} collective-permute-done((bf16[16,4096]{1,0:T(8,128)(2,1)S(1)}, bf16[16,4096]{1,0:T(8,128)(2,1)S(1)}, u32[]{:S(2)}, u32[]{:S(2)}) %collective-permute-start.34) | collective-permute-done | bytes 131104 | tf_op jit(solution)/shard_map/ppermute | solution.py:71
  (90 shorter events, 42.6 us)
Async XLA Ops:
  7.1 27.7 %collective-permute-start = (bf16[1056,128]{1,0:T(8,128)(2,1)}, bf16[1056,128]{1,0:T(8,128)(2,1)S(1)}, u32[]{:S(2)}, u32[]{:S(2)}) collective-permute-start(bf16[1056,128]{1,0:T(8,128)(2,1)} %attention.4), channel_id=1, source_target_pairs={{0,8},{4,12},{8,0},{12,4},{1,9},{5,13},{9,1},{13,5},{2,10},{6,14},... | collective-permute-start | bytes 811016 | tf_op jit(solution)/shard_map/ppermute | solution.py:71
  17.7 17.1 %collective-permute-start.1 = (bf16[1056,128]{1,0:T(8,128)(2,1)}, bf16[1056,128]{1,0:T(8,128)(2,1)S(1)}, u32[]{:S(2)}, u32[]{:S(2)}) collective-permute-start(bf16[1056,128]{1,0:T(8,128)(2,1)} %attention.5), channel_id=1, source_target_pairs={{0,4},{4,8},{8,12},{12,0},{1,5},{5,9},{9,13},{13,1},{2,6},{6,10},{... | collective-permute-start | bytes 811016 | tf_op jit(solution)/shard_map/ppermute | solution.py:71
  25.8 9.5 %collective-permute-start.2 = (bf16[1056,128]{1,0:T(8,128)(2,1)}, bf16[1056,128]{1,0:T(8,128)(2,1)S(1)}, u32[]{:S(2)}, u32[]{:S(2)}) collective-permute-start(bf16[1056,128]{1,0:T(8,128)(2,1)} %attention.6), channel_id=1, source_target_pairs={{0,12},{4,0},{8,4},{12,8},{1,13},{5,1},{9,5},{13,9},{2,14},{6,2},{... | collective-permute-start | bytes 811016 | tf_op jit(solution)/shard_map/ppermute | solution.py:71
  51.9 10.7 %collective-permute-start.5 = (bf16[16,4096]{1,0:T(8,128)(2,1)S(1)}, bf16[16,4096]{1,0:T(8,128)(2,1)S(1)}, u32[]{:S(2)}, u32[]{:S(2)}) collective-permute-start(bf16[16,4096]{1,0:T(8,128)(2,1)S(1)} %get-tuple-element.35), channel_id=1, source_target_pairs={{0,8},{4,12},{8,0},{12,4},{1,9},{5,13},{9,1},{13,5},{2,10},{6,14},... | collective-permute-start | bytes 393224 | tf_op jit(solution)/shard_map/ppermute | solution.py:71
  55.9 9.5 %collective-permute-start.7 = (bf16[16,4096]{1,0:T(8,128)(2,1)S(1)}, bf16[16,4096]{1,0:T(8,128)(2,1)S(1)}, u32[]{:S(2)}, u32[]{:S(2)}) collective-permute-start(bf16[16,4096]{1,0:T(8,128)(2,1)S(1)} %get-tuple-element.37), channel_id=1, source_target_pairs={{0,4},{4,8},{8,12},{12,0},{1,5},{5,9},{9,13},{13,1},{2,6},{6,10},{... | collective-permute-start | bytes 393224 | tf_op jit(solution)/shard_map/ppermute | solution.py:71
  68.4 13.8 %collective-permute-start.9 = (bf16[16,4224]{1,0:T(8,128)(2,1)S(1)}, bf16[16,4224]{1,0:T(8,128)(2,1)S(1)}, u32[]{:S(2)}, u32[]{:S(2)}) collective-permute-start(bf16[16,4224]{1,0:T(8,128)(2,1)S(1)} %get-tuple-element.38.refs_0_), channel_id=1, source_target_pairs={{0,8},{4,12},{8,0},{12,4},{1,9},{5,13},{9,1},{13,5},{2,10},{6,14},... | collective-permute-start | bytes 405512 | tf_op jit(solution)/shard_map/ppermute | solution.py:71
  70.1 12.1 %collective-permute-start.8 = (bf16[16,4224]{1,0:T(8,128)(2,1)S(1)}, bf16[16,4224]{1,0:T(8,128)(2,1)S(1)}, u32[]{:S(2)}, u32[]{:S(2)}) collective-permute-start(bf16[16,4224]{1,0:T(8,128)(2,1)S(1)} %get-tuple-element.38.refs_0_), channel_id=1, source_target_pairs={{0,4},{4,8},{8,12},{12,0},{1,5},{5,9},{9,13},{13,1},{2,6},{6,10},{... | collective-permute-start | bytes 405512 | tf_op jit(solution)/shard_map/ppermute | solution.py:71
  72.0 10.3 %collective-permute-start.12 = (bf16[64,4096]{1,0:T(8,128)(2,1)S(1)}, bf16[64,4096]{1,0:T(8,128)(2,1)S(1)}, u32[]{:S(2)}, u32[]{:S(2)}) collective-permute-start(bf16[64,4096]{1,0:T(8,128)(2,1)S(1)} %get-tuple-element.59), channel_id=1, source_target_pairs={{0,1},{1,0},{2,3},{3,2},{4,5},{5,4},{6,7},{7,6},{8,9},{9,8},{10,11... | collective-permute-start | bytes 1572872 | tf_op jit(solution)/shard_map/ppermute | solution.py:71
  82.5 10.8 %collective-permute-start.13 = (bf16[16,4096]{1,0:T(8,128)(2,1)S(1)}, bf16[16,4096]{1,0:T(8,128)(2,1)S(1)}, u32[]{:S(2)}, u32[]{:S(2)}) collective-permute-start(bf16[16,4096]{1,0:T(8,128)(2,1)S(1)} %get-tuple-element.42), channel_id=1, source_target_pairs={{0,8},{4,12},{8,0},{12,4},{1,9},{5,13},{9,1},{13,5},{2,10},{6,14},... | collective-permute-start | bytes 393224 | tf_op jit(solution)/shard_map/ppermute | solution.py:71
  83.4 11.2 %collective-permute-start.14 = (bf16[16,4096]{1,0:T(8,128)(2,1)S(1)}, bf16[16,4096]{1,0:T(8,128)(2,1)S(1)}, u32[]{:S(2)}, u32[]{:S(2)}) collective-permute-start(bf16[16,4096]{1,0:T(8,128)(2,1)S(1)} %get-tuple-element.43), channel_id=1, source_target_pairs={{0,12},{4,0},{8,4},{12,8},{1,13},{5,1},{9,5},{13,9},{2,14},{6,2},{... | collective-permute-start | bytes 393224 | tf_op jit(solution)/shard_map/ppermute | solution.py:71
  83.8 10.8 %collective-permute-start.15 = (bf16[16,4096]{1,0:T(8,128)(2,1)S(1)}, bf16[16,4096]{1,0:T(8,128)(2,1)S(1)}, u32[]{:S(2)}, u32[]{:S(2)}) collective-permute-start(bf16[16,4096]{1,0:T(8,128)(2,1)S(1)} %get-tuple-element.44), channel_id=1, source_target_pairs={{0,4},{4,8},{8,12},{12,0},{1,5},{5,9},{9,13},{13,1},{2,6},{6,10},{... | collective-permute-start | bytes 393224 | tf_op jit(solution)/shard_map/ppermute | solution.py:71
  91.8 14.2 %collective-permute-start.16 = (bf16[128,2176]{1,0:T(8,128)(2,1)S(1)}, bf16[128,2176]{1,0:T(8,128)(2,1)S(1)}, u32[]{:S(2)}, u32[]{:S(2)}) collective-permute-start(bf16[128,2176]{1,0:T(8,128)(2,1)S(1)} %gate_up.4.refs_6_), channel_id=1, source_target_pairs={{0,2},{2,0},{1,3},{3,1},{4,6},{6,4},{5,7},{7,5},{8,10},{10,8},{9,1... | collective-permute-start | bytes 1671176 | tf_op jit(solution)/shard_map/ppermute | solution.py:71
  94.8 15.4 %collective-permute-start.20 = (bf16[16,4224]{1,0:T(8,128)(2,1)S(1)}, bf16[16,4224]{1,0:T(8,128)(2,1)S(1)}, u32[]{:S(2)}, u32[]{:S(2)}) collective-permute-start(bf16[16,4224]{1,0:T(8,128)(2,1)S(1)} %get-tuple-element.46.refs_0_), channel_id=1, source_target_pairs={{0,12},{4,0},{8,4},{12,8},{1,13},{5,1},{9,5},{13,9},{2,14},{6,2},{... | collective-permute-start | bytes 405512 | tf_op jit(solution)/shard_map/ppermute | solution.py:71
  95.8 14.8 %collective-permute-start.19 = (bf16[16,4224]{1,0:T(8,128)(2,1)S(1)}, bf16[16,4224]{1,0:T(8,128)(2,1)S(1)}, u32[]{:S(2)}, u32[]{:S(2)}) collective-permute-start(bf16[16,4224]{1,0:T(8,128)(2,1)S(1)} %get-tuple-element.46.refs_0_), channel_id=1, source_target_pairs={{0,8},{4,12},{8,0},{12,4},{1,9},{5,13},{9,1},{13,5},{2,10},{6,14},... | collective-permute-start | bytes 405512 | tf_op jit(solution)/shard_map/ppermute | solution.py:71
  98.4 12.2 %collective-permute-start.18 = (bf16[16,4224]{1,0:T(8,128)(2,1)S(1)}, bf16[16,4224]{1,0:T(8,128)(2,1)S(1)}, u32[]{:S(2)}, u32[]{:S(2)}) collective-permute-start(bf16[16,4224]{1,0:T(8,128)(2,1)S(1)} %get-tuple-element.46.refs_0_), channel_id=1, source_target_pairs={{0,4},{4,8},{8,12},{12,0},{1,5},{5,9},{9,13},{13,1},{2,6},{6,10},{... | collective-permute-start | bytes 405512 | tf_op jit(solution)/shard_map/ppermute | solution.py:71
  110.7 16.2 %collective-permute-start.17 = (bf16[128,1024]{1,0:T(8,128)(2,1)S(1)}, bf16[128,1024]{1,0:T(8,128)(2,1)S(1)}, u32[]{:S(2)}, u32[]{:S(2)}) collective-permute-start(bf16[128,1024]{1,0:T(8,128)(2,1)S(1)} %activate.2.refs_1_.refs_3_), channel_id=1, source_target_pairs={{0,2},{2,0},{1,3},{3,1},{4,6},{6,4},{5,7},{7,5},{8,10},{10,8},{9,1... | collective-permute-start | bytes 786440 | tf_op jit(solution)/shard_map/ppermute | solution.py:71
  119.0 14.7 %collective-permute-start.23 = (bf16[128,2176]{1,0:T(8,128)(2,1)S(1)}, bf16[128,2176]{1,0:T(8,128)(2,1)S(1)}, u32[]{:S(2)}, u32[]{:S(2)}) collective-permute-start(bf16[128,2176]{1,0:T(8,128)(2,1)S(1)} %gate_up.6.refs_5_), channel_id=1, source_target_pairs={{0,2},{2,0},{1,3},{3,1},{4,6},{6,4},{5,7},{7,5},{8,10},{10,8},{9,1... | collective-permute-start | bytes 1671176 | tf_op jit(solution)/shard_map/ppermute | solution.py:71
  134.1 9.4 %collective-permute-start.27 = (bf16[128,1024]{1,0:T(8,128)(2,1)S(1)}, bf16[128,1024]{1,0:T(8,128)(2,1)S(1)}, u32[]{:S(2)}, u32[]{:S(2)}) collective-permute-start(bf16[128,1024]{1,0:T(8,128)(2,1)S(1)} %activate.3.refs_2_.refs_1_.refs_3_), channel_id=1, source_target_pairs={{0,2},{2,0},{1,3},{3,1},{4,6},{6,4},{5,7},{7,5},{8,10},{10,8},{9,1... | collective-permute-start | bytes 786440 | tf_op jit(solution)/shard_map/ppermute | solution.py:71
  135.8 12.3 %collective-permute-start.24 = (bf16[16,4096]{1,0:T(8,128)(2,1)S(1)}, bf16[16,4096]{1,0:T(8,128)(2,1)S(1)}, u32[]{:S(2)}, u32[]{:S(2)}) collective-permute-start(bf16[16,4096]{1,0:T(8,128)(2,1)S(1)} %get-tuple-element.49), channel_id=1, source_target_pairs={{0,4},{4,8},{8,12},{12,0},{1,5},{5,9},{9,13},{13,1},{2,6},{6,10},{... | collective-permute-start | bytes 393224 | tf_op jit(solution)/shard_map/ppermute | solution.py:71
  136.4 11.7 %collective-permute-start.25 = (bf16[16,4096]{1,0:T(8,128)(2,1)S(1)}, bf16[16,4096]{1,0:T(8,128)(2,1)S(1)}, u32[]{:S(2)}, u32[]{:S(2)}) collective-permute-start(bf16[16,4096]{1,0:T(8,128)(2,1)S(1)} %get-tuple-element.50), channel_id=1, source_target_pairs={{0,12},{4,0},{8,4},{12,8},{1,13},{5,1},{9,5},{13,9},{2,14},{6,2},{... | collective-permute-start | bytes 393224 | tf_op jit(solution)/shard_map/ppermute | solution.py:71
  139.6 10.5 %collective-permute-start.26 = (bf16[16,4096]{1,0:T(8,128)(2,1)S(1)}, bf16[16,4096]{1,0:T(8,128)(2,1)S(1)}, u32[]{:S(2)}, u32[]{:S(2)}) collective-permute-start(bf16[16,4096]{1,0:T(8,128)(2,1)S(1)} %get-tuple-element.51), channel_id=1, source_target_pairs={{0,8},{4,12},{8,0},{12,4},{1,9},{5,13},{9,1},{13,5},{2,10},{6,14},... | collective-permute-start | bytes 393224 | tf_op jit(solution)/shard_map/ppermute | solution.py:71
  150.4 8.3 %collective-permute-start.32 = (bf16[16,4096]{1,0:T(8,128)(2,1)S(1)}, bf16[16,4096]{1,0:T(8,128)(2,1)S(1)}, u32[]{:S(2)}, u32[]{:S(2)}) collective-permute-start(bf16[16,4096]{1,0:T(8,128)(2,1)S(1)} %get-tuple-element.55), channel_id=1, source_target_pairs={{0,4},{4,8},{8,12},{12,0},{1,5},{5,9},{9,13},{13,1},{2,6},{6,10},{... | collective-permute-start | bytes 393224 | tf_op jit(solution)/shard_map/ppermute | solution.py:71
  150.8 9.0 %collective-permute-start.33 = (bf16[16,4096]{1,0:T(8,128)(2,1)S(1)}, bf16[16,4096]{1,0:T(8,128)(2,1)S(1)}, u32[]{:S(2)}, u32[]{:S(2)}) collective-permute-start(bf16[16,4096]{1,0:T(8,128)(2,1)S(1)} %get-tuple-element.56), channel_id=1, source_target_pairs={{0,12},{4,0},{8,4},{12,8},{1,13},{5,1},{9,5},{13,9},{2,14},{6,2},{... | collective-permute-start | bytes 393224 | tf_op jit(solution)/shard_map/ppermute | solution.py:71
  154.3 11.4 %collective-permute-start.34 = (bf16[16,4096]{1,0:T(8,128)(2,1)S(1)}, bf16[16,4096]{1,0:T(8,128)(2,1)S(1)}, u32[]{:S(2)}, u32[]{:S(2)}) collective-permute-start(bf16[16,4096]{1,0:T(8,128)(2,1)S(1)} %get-tuple-element.57), channel_id=1, source_target_pairs={{0,8},{4,12},{8,0},{12,4},{1,9},{5,13},{9,1},{13,5},{2,10},{6,14},... | collective-permute-start | bytes 393224 | tf_op jit(solution)/shard_map/ppermute | solution.py:71
  (15 other events, 112.7 us)
